TPU v7x, 512 devices: a whole 4x8x8 slice. The times are simulated.
512 devices in a mesh: section: 8 (over y_lo, x), ctx: 64 (over y_hi, z, core).
Axes of the slice: x: 4, y: 8 (y_hi: 4, y_lo: 2; y = y_hi * 2 + y_lo), z: 8, core: 2. Of those that a mesh axis runs over, the one named last changes fastest.
Arguments:
- x_in: bfloat16 [2048, 1536], P('ctx'), may hold values from -6 to 6
- stale_inputs: bfloat16 [8, 2048, 1536], P('section', 'ctx'), may hold values from -6 to 6
- w_query: bfloat16 [8, 12, 128, 128], P('section'), may hold values from -0.5 to 0.5
- w_key: bfloat16 [8, 12, 128, 128], P('section'), may hold values from -0.5 to 0.5
- w_value: bfloat16 [8, 12, 128, 128], P('section'), may hold values from -0.5 to 0.5
- w_out: bfloat16 [8, 12, 128, 128], P('section'), may hold values from -0.5 to 0.5
- score_scale: float32 [8, 12], P('section'), may hold values from 1 to 3
- assign: int32 [2048], P('ctx'), may hold values from 0 to 3, as said below
Outputs:
- section_out: bfloat16 [8, 2048, 1536], P('section', 'ctx')
Inputs may be any that keep to these rules, and one draw needn't show every extreme that they name: `assign`: each aligned block of 32 tokens holds the same number of tokens of every micro-batch.
All inputs are finite; a program needn't handle non-finite values.
Results may differ from a plain program's by a relative error of at most 0.013.
Values may be sent and summed in bfloat16 or wider, within the bound.
A program may use at most 128 MiB of HBM per device.

v0:
```python
import math

import jax
import jax.numpy as jnp
from jax import lax
from jax.sharding import PartitionSpec as P

MB = 4


def from_behind(array, axis, by):
    length = lax.axis_size(axis)
    pairs = [(i, i + by) for i in range(length) if 0 <= i + by < length]
    return lax.ppermute(array, axis, pairs)


def normalize(values):
    floats = values.astype(jnp.float32)
    return floats * lax.rsqrt(jnp.mean(floats * floats, axis=-1, keepdims=True) + 1e-06)


def project(normed, weight):
    count = normed.shape[0]
    return jnp.einsum(
        "nhd,hde->nhe",
        normed.reshape(count, weight.shape[0], weight.shape[1]),
        weight,
        preferred_element_type=jnp.float32,
    )


def key_pair(normed, w_key, w_value):
    count = normed.shape[0]
    keys = normalize(project(normed, w_key)).astype(jnp.bfloat16).reshape(count, -1)
    values = project(normed, w_value).astype(jnp.bfloat16).reshape(count, -1)
    return jnp.stack([keys, values])


def body(x_in, stale_inputs, w_query, w_key, w_value, w_out, score_scale, assign):
    tile_rows = x_in.shape[0]
    feature_width = x_in.shape[1]
    heads = w_query.shape[1]
    head_size = w_query.shape[2]
    query_weight = w_query[0]
    key_weight = w_key[0]
    value_weight = w_value[0]
    mix_weight = w_out[0]
    scales = score_scale[0]
    sections = lax.axis_size("section")
    section_index = lax.axis_index("section")
    ctx_index = lax.axis_index("ctx")
    per_batch = tile_rows // MB
    stale_normed = normalize(stale_inputs[0]).astype(jnp.bfloat16)
    pairs = lax.all_gather(
        key_pair(stale_normed, key_weight, value_weight), "ctx", axis=1, tiled=True
    )
    total = pairs.shape[1]
    far_keys = pairs[0].reshape(total, heads, head_size)
    far_values = pairs[1].reshape(total, heads, head_size)
    own_pair = lax.dynamic_slice_in_dim(pairs, ctx_index * tile_rows, tile_rows, 1)
    own_keys = own_pair[0].reshape(tile_rows, heads, head_size)
    own_values = own_pair[1].reshape(tile_rows, heads, head_size)
    far_mask = (jnp.arange(total, dtype=jnp.int32) // tile_rows != ctx_index).astype(jnp.float32)
    order = jnp.argsort(assign, stable=True)

    def advance(entering, batch_index, fresh_keys, fresh_values, rows):
        normed = normalize(entering).astype(jnp.bfloat16)
        queries = (
            normalize(project(normed, query_weight))
            * (scales[None, :, None] / math.sqrt(head_size))
        ).astype(jnp.bfloat16)
        new_keys = normalize(project(normed, key_weight)).astype(jnp.bfloat16)
        new_values = project(normed, value_weight).astype(jnp.bfloat16)
        fresh_keys = fresh_keys.at[rows].set(new_keys)
        fresh_values = fresh_values.at[rows].set(new_values)
        chosen = (assign <= batch_index).astype(jnp.float32)
        e_far = (
            jnp.exp(
                jnp.einsum("qhd,khd->hqk", queries, far_keys, preferred_element_type=jnp.float32)
            )
            * far_mask[None, None, :]
        )
        e_new = (
            jnp.exp(
                jnp.einsum("qhd,khd->hqk", queries, fresh_keys, preferred_element_type=jnp.float32)
            )
            * chosen[None, None, :]
        )
        e_old = (
            jnp.exp(
                jnp.einsum("qhd,khd->hqk", queries, own_keys, preferred_element_type=jnp.float32)
            )
            * (1.0 - chosen)[None, None, :]
        )
        denom = jnp.sum(e_far, -1) + jnp.sum(e_new, -1) + jnp.sum(e_old, -1)
        numer = jnp.einsum(
            "hqk,khd->qhd",
            e_far.astype(jnp.bfloat16),
            far_values,
            preferred_element_type=jnp.float32,
        )
        numer = numer + jnp.einsum(
            "hqk,khd->qhd",
            e_new.astype(jnp.bfloat16),
            fresh_values,
            preferred_element_type=jnp.float32,
        )
        numer = numer + jnp.einsum(
            "hqk,khd->qhd",
            e_old.astype(jnp.bfloat16),
            own_values,
            preferred_element_type=jnp.float32,
        )
        attended = (
            (numer / jnp.transpose(denom)[:, :, None])
            .astype(jnp.bfloat16)
            .reshape(per_batch, feature_width)
        )
        mixed = project(attended, mix_weight).reshape(per_batch, feature_width)
        return (
            (entering.astype(jnp.float32) + mixed).astype(jnp.bfloat16),
            fresh_keys,
            fresh_values,
        )

    def advance_step(moment, carry):
        incoming, out_buffer, fresh_keys, fresh_values = carry
        batch_index = moment - section_index
        valid = jnp.logical_and(batch_index >= 0, batch_index < MB)
        clamped = jnp.clip(batch_index, 0, MB - 1)
        rows = lax.dynamic_slice_in_dim(order, clamped * per_batch, per_batch)
        entering = jnp.where(section_index == 0, x_in[rows], incoming)
        result, next_keys, next_values = advance(entering, clamped, fresh_keys, fresh_values, rows)
        next_keys = jnp.where(valid, next_keys, fresh_keys)
        next_values = jnp.where(valid, next_values, fresh_values)
        out_buffer = jnp.where(valid, out_buffer.at[rows].set(result), out_buffer)
        incoming = from_behind(result, "section", 1)
        return (incoming, out_buffer, next_keys, next_values)

    initial = (
        jnp.zeros((per_batch, feature_width), jnp.bfloat16),
        jnp.zeros_like(x_in),
        jnp.zeros((tile_rows, heads, head_size), jnp.bfloat16),
        jnp.zeros((tile_rows, heads, head_size), jnp.bfloat16),
    )
    final = lax.fori_loop(0, MB + sections - 1, advance_step, initial)
    return final[1][None]


def solution(mesh):
    return jax.shard_map(
        body,
        mesh=mesh,
        in_specs=(
            P("ctx", None),
            P("section", "ctx", None),
            P("section", None, None, None),
            P("section", None, None, None),
            P("section", None, None, None),
            P("section", None, None, None),
            P("section", None),
            P("ctx"),
        ),
        out_specs=P("section", "ctx", None),
        check_vma=False,
    )
```

profile of v0, /device:TPU:8, one launch (start us, length us, event | category | flops | bytes accessed | tf_op | source)
XLA Modules:
  0.0 420.3 jit_solution(3369627692804567178)
XLA Ops:
  12.4 2.3 sort.17
  14.6 124.3 %all-gather.2.cloned.1.call-done = bf16[2,2048,1536]{2,1,0:T(8,128)(2,1)} async-done(((bf16[2,32,1536]{2,1,0:T(8,128)(2,1)}), bf16[2,2048,1536]{2,1,0:T(8,128)(2,1)}) %all-gather.2.cloned.1.call-update) | async-done | bytes 12582928 | tf_op jit(solution)/shard_map/all_gather | solution.py:54
  140.1 10.3 %fusion.39 = (bf16[1,2048,1536]{2,1,0:T(8,128)(2,1)}, bf16[1,2048,1536]{2,1,0:T(8,128)(2,1)}) fusion(bf16[2,2048,1536]{2,1,0:T(8,128)(2,1)} %all-gather.2.cloned.1.call-done), kind=kLoop, calls=%fused_computation.83 | loop fusion | bytes 25165824 | tf_op jit(solution)/shard_map/slice | solution.py:59
  150.4 8.7 %copy.32 = bf16[1,2048,1536]{1,2,0:T(8,128)(2,1)} copy(bf16[1,2048,1536]{2,1,0:T(8,128)(2,1)} %get-tuple-element.558) | data formatting | bytes 12582912 | tf_op jit(solution)/shard_map/slice | solution.py:58
  159.1 8.7 %copy.34 = bf16[2048,12,128]{2,0,1:T(8,128)(2,1)} copy(bf16[2048,12,128]{0,2,1:T(8,128)(2,1)} %bitcast.122) | data formatting | bytes 12582912
  167.7 8.7 %copy.33 = bf16[1,2048,1536]{1,2,0:T(8,128)(2,1)} copy(bf16[1,2048,1536]{2,1,0:T(8,128)(2,1)} %get-tuple-element.557) | data formatting | bytes 12582912 | tf_op jit(solution)/shard_map/slice | solution.py:59
  176.5 8.7 %copy.35 = bf16[2048,12,128]{2,0,1:T(8,128)(2,1)} copy(bf16[2048,12,128]{0,2,1:T(8,128)(2,1)} %bitcast.123) | data formatting | bytes 12582912
  185.3 227.5 %while.21 = (s32[]{:T(128)}, bf16[8,1536]{1,0:T(8,128)(2,1)S(1)}, bf16[32,1536]{1,0:T(8,128)(2,1)S(1)}, bf16[32,12,128]{2,1,0:T(8,128)(2,1)S(1)}, bf16[32,12,128...) while((s32[]{:T(128)}, bf16[8,1536]{1,0:T(8,128)(2,1)S(1)}, ...), condition=%wide.region_13.14_spmd.clone, body=%wide.region_3.13_spmd.clone.sunk | while | flops 117734640 | bytes 18460220 | solution.py:146
  188.4 4.6 %fusion.96 = (f32[12,8]{1,0:T(8,128)S(1)}, bf16[12,8,2048]{2,1,0:T(8,128)(2,1)S(1)}) fusion(f32[2048]{0:T(1024)S(1)} %fusion.94, bf16[8,12,128]{2,0,1:T(8,128)(2,1)S(1)} %multiply_convert_fusion.5, bf16[2048,12,128]{2,0,1:T(8,128)(2,1)} %get-tuple-element.783), kind=kOutput, calls=%fused_computation.81.clone.1 | convolution fusion | flops 50921376 | bytes 6717824 | tf_op jit(solution)/shard_map/while/body/eval_jaxpr/qhd,khd->hqk/dot_general | solution.py:79
  194.0 3.7 convolution_bitcast_fusion.8
  198.2 3.4 collective-permute-start
  202.4 3.6 collective-permute-done
  209.1 4.6 %fusion.96 = (f32[12,8]{1,0:T(8,128)S(1)}, bf16[12,8,2048]{2,1,0:T(8,128)(2,1)S(1)}) fusion(f32[2048]{0:T(1024)S(1)} %fusion.94, bf16[8,12,128]{2,0,1:T(8,128)(2,1)S(1)} %multiply_convert_fusion.5, bf16[2048,12,128]{2,0,1:T(8,128)(2,1)} %get-tuple-element.783), kind=kOutput, calls=%fused_computation.81.clone.1 | convolution fusion | flops 50921376 | bytes 6717824 | tf_op jit(solution)/shard_map/while/body/eval_jaxpr/qhd,khd->hqk/dot_general | solution.py:79
  214.7 3.7 convolution_bitcast_fusion.8
  218.9 1.9 collective-permute-start
  221.7 5.0 %collective-permute-done = bf16[8,1536]{1,0:T(8,128)(2,1)S(1)} collective-permute-done((bf16[8,1536]{1,0:T(8,128)(2,1)S(1)}, bf16[8,1536]{1,0:T(8,128)(2,1)S(1)}, u32[]{:S(2)}, u32[]{:S(2)}) %collective-permute-start) | collective-permute-done | bytes 24608 | tf_op jit(solution)/shard_map/while/body/eval_jaxpr/ppermute | solution.py:14
  229.7 4.6 %fusion.96 = (f32[12,8]{1,0:T(8,128)S(1)}, bf16[12,8,2048]{2,1,0:T(8,128)(2,1)S(1)}) fusion(f32[2048]{0:T(1024)S(1)} %fusion.94, bf16[8,12,128]{2,0,1:T(8,128)(2,1)S(1)} %multiply_convert_fusion.5, bf16[2048,12,128]{2,0,1:T(8,128)(2,1)} %get-tuple-element.783), kind=kOutput, calls=%fused_computation.81.clone.1 | convolution fusion | flops 50921376 | bytes 6717824 | tf_op jit(solution)/shard_map/while/body/eval_jaxpr/qhd,khd->hqk/dot_general | solution.py:79
  235.3 3.7 convolution_bitcast_fusion.8
  239.5 1.9 collective-permute-start
  242.3 5.0 %collective-permute-done = bf16[8,1536]{1,0:T(8,128)(2,1)S(1)} collective-permute-done((bf16[8,1536]{1,0:T(8,128)(2,1)S(1)}, bf16[8,1536]{1,0:T(8,128)(2,1)S(1)}, u32[]{:S(2)}, u32[]{:S(2)}) %collective-permute-start) | collective-permute-done | bytes 24608 | tf_op jit(solution)/shard_map/while/body/eval_jaxpr/ppermute | solution.py:14
  250.4 4.6 %fusion.96 = (f32[12,8]{1,0:T(8,128)S(1)}, bf16[12,8,2048]{2,1,0:T(8,128)(2,1)S(1)}) fusion(f32[2048]{0:T(1024)S(1)} %fusion.94, bf16[8,12,128]{2,0,1:T(8,128)(2,1)S(1)} %multiply_convert_fusion.5, bf16[2048,12,128]{2,0,1:T(8,128)(2,1)} %get-tuple-element.783), kind=kOutput, calls=%fused_computation.81.clone.1 | convolution fusion | flops 50921376 | bytes 6717824 | tf_op jit(solution)/shard_map/while/body/eval_jaxpr/qhd,khd->hqk/dot_general | solution.py:79
  256.0 3.7 convolution_bitcast_fusion.8
  260.2 1.9 collective-permute-start
  263.0 5.0 %collective-permute-done = bf16[8,1536]{1,0:T(8,128)(2,1)S(1)} collective-permute-done((bf16[8,1536]{1,0:T(8,128)(2,1)S(1)}, bf16[8,1536]{1,0:T(8,128)(2,1)S(1)}, u32[]{:S(2)}, u32[]{:S(2)}) %collective-permute-start) | collective-permute-done | bytes 24608 | tf_op jit(solution)/shard_map/while/body/eval_jaxpr/ppermute | solution.py:14
  271.1 4.6 %fusion.96 = (f32[12,8]{1,0:T(8,128)S(1)}, bf16[12,8,2048]{2,1,0:T(8,128)(2,1)S(1)}) fusion(f32[2048]{0:T(1024)S(1)} %fusion.94, bf16[8,12,128]{2,0,1:T(8,128)(2,1)S(1)} %multiply_convert_fusion.5, bf16[2048,12,128]{2,0,1:T(8,128)(2,1)} %get-tuple-element.783), kind=kOutput, calls=%fused_computation.81.clone.1 | convolution fusion | flops 50921376 | bytes 6717824 | tf_op jit(solution)/shard_map/while/body/eval_jaxpr/qhd,khd->hqk/dot_general | solution.py:79
  276.7 3.7 convolution_bitcast_fusion.8
  280.9 1.9 collective-permute-start
  283.7 5.0 %collective-permute-done = bf16[8,1536]{1,0:T(8,128)(2,1)S(1)} collective-permute-done((bf16[8,1536]{1,0:T(8,128)(2,1)S(1)}, bf16[8,1536]{1,0:T(8,128)(2,1)S(1)}, u32[]{:S(2)}, u32[]{:S(2)}) %collective-permute-start) | collective-permute-done | bytes 24608 | tf_op jit(solution)/shard_map/while/body/eval_jaxpr/ppermute | solution.py:14
  291.8 4.6 %fusion.96 = (f32[12,8]{1,0:T(8,128)S(1)}, bf16[12,8,2048]{2,1,0:T(8,128)(2,1)S(1)}) fusion(f32[2048]{0:T(1024)S(1)} %fusion.94, bf16[8,12,128]{2,0,1:T(8,128)(2,1)S(1)} %multiply_convert_fusion.5, bf16[2048,12,128]{2,0,1:T(8,128)(2,1)} %get-tuple-element.783), kind=kOutput, calls=%fused_computation.81.clone.1 | convolution fusion | flops 50921376 | bytes 6717824 | tf_op jit(solution)/shard_map/while/body/eval_jaxpr/qhd,khd->hqk/dot_general | solution.py:79
  297.4 3.7 convolution_bitcast_fusion.8
  301.6 1.9 collective-permute-start
  304.4 5.0 %collective-permute-done = bf16[8,1536]{1,0:T(8,128)(2,1)S(1)} collective-permute-done((bf16[8,1536]{1,0:T(8,128)(2,1)S(1)}, bf16[8,1536]{1,0:T(8,128)(2,1)S(1)}, u32[]{:S(2)}, u32[]{:S(2)}) %collective-permute-start) | collective-permute-done | bytes 24608 | tf_op jit(solution)/shard_map/while/body/eval_jaxpr/ppermute | solution.py:14
  312.5 4.6 %fusion.96 = (f32[12,8]{1,0:T(8,128)S(1)}, bf16[12,8,2048]{2,1,0:T(8,128)(2,1)S(1)}) fusion(f32[2048]{0:T(1024)S(1)} %fusion.94, bf16[8,12,128]{2,0,1:T(8,128)(2,1)S(1)} %multiply_convert_fusion.5, bf16[2048,12,128]{2,0,1:T(8,128)(2,1)} %get-tuple-element.783), kind=kOutput, calls=%fused_computation.81.clone.1 | convolution fusion | flops 50921376 | bytes 6717824 | tf_op jit(solution)/shard_map/while/body/eval_jaxpr/qhd,khd->hqk/dot_general | solution.py:79
  318.1 3.7 convolution_bitcast_fusion.8
  322.3 1.9 collective-permute-start
  325.1 5.0 %collective-permute-done = bf16[8,1536]{1,0:T(8,128)(2,1)S(1)} collective-permute-done((bf16[8,1536]{1,0:T(8,128)(2,1)S(1)}, bf16[8,1536]{1,0:T(8,128)(2,1)S(1)}, u32[]{:S(2)}, u32[]{:S(2)}) %collective-permute-start) | collective-permute-done | bytes 24608 | tf_op jit(solution)/shard_map/while/body/eval_jaxpr/ppermute | solution.py:14
  333.2 4.6 %fusion.96 = (f32[12,8]{1,0:T(8,128)S(1)}, bf16[12,8,2048]{2,1,0:T(8,128)(2,1)S(1)}) fusion(f32[2048]{0:T(1024)S(1)} %fusion.94, bf16[8,12,128]{2,0,1:T(8,128)(2,1)S(1)} %multiply_convert_fusion.5, bf16[2048,12,128]{2,0,1:T(8,128)(2,1)} %get-tuple-element.783), kind=kOutput, calls=%fused_computation.81.clone.1 | convolution fusion | flops 50921376 | bytes 6717824 | tf_op jit(solution)/shard_map/while/body/eval_jaxpr/qhd,khd->hqk/dot_general | solution.py:79
  338.8 3.7 convolution_bitcast_fusion.8
  345.7 5.0 %collective-permute-done = bf16[8,1536]{1,0:T(8,128)(2,1)S(1)} collective-permute-done((bf16[8,1536]{1,0:T(8,128)(2,1)S(1)}, bf16[8,1536]{1,0:T(8,128)(2,1)S(1)}, u32[]{:S(2)}, u32[]{:S(2)}) %collective-permute-start) | collective-permute-done | bytes 24608 | tf_op jit(solution)/shard_map/while/body/eval_jaxpr/ppermute | solution.py:14
  353.8 4.6 %fusion.96 = (f32[12,8]{1,0:T(8,128)S(1)}, bf16[12,8,2048]{2,1,0:T(8,128)(2,1)S(1)}) fusion(f32[2048]{0:T(1024)S(1)} %fusion.94, bf16[8,12,128]{2,0,1:T(8,128)(2,1)S(1)} %multiply_convert_fusion.5, bf16[2048,12,128]{2,0,1:T(8,128)(2,1)} %get-tuple-element.783), kind=kOutput, calls=%fused_computation.81.clone.1 | convolution fusion | flops 50921376 | bytes 6717824 | tf_op jit(solution)/shard_map/while/body/eval_jaxpr/qhd,khd->hqk/dot_general | solution.py:79
  359.4 3.7 convolution_bitcast_fusion.8
  366.4 5.0 %collective-permute-done = bf16[8,1536]{1,0:T(8,128)(2,1)S(1)} collective-permute-done((bf16[8,1536]{1,0:T(8,128)(2,1)S(1)}, bf16[8,1536]{1,0:T(8,128)(2,1)S(1)}, u32[]{:S(2)}, u32[]{:S(2)}) %collective-permute-start) | collective-permute-done | bytes 24608 | tf_op jit(solution)/shard_map/while/body/eval_jaxpr/ppermute | solution.py:14
  374.5 4.6 %fusion.96 = (f32[12,8]{1,0:T(8,128)S(1)}, bf16[12,8,2048]{2,1,0:T(8,128)(2,1)S(1)}) fusion(f32[2048]{0:T(1024)S(1)} %fusion.94, bf16[8,12,128]{2,0,1:T(8,128)(2,1)S(1)} %multiply_convert_fusion.5, bf16[2048,12,128]{2,0,1:T(8,128)(2,1)} %get-tuple-element.783), kind=kOutput, calls=%fused_computation.81.clone.1 | convolution fusion | flops 50921376 | bytes 6717824 | tf_op jit(solution)/shard_map/while/body/eval_jaxpr/qhd,khd->hqk/dot_general | solution.py:79
  380.1 3.7 convolution_bitcast_fusion.8
  387.1 5.0 %collective-permute-done = bf16[8,1536]{1,0:T(8,128)(2,1)S(1)} collective-permute-done((bf16[8,1536]{1,0:T(8,128)(2,1)S(1)}, bf16[8,1536]{1,0:T(8,128)(2,1)S(1)}, u32[]{:S(2)}, u32[]{:S(2)}) %collective-permute-start) | collective-permute-done | bytes 24608 | tf_op jit(solution)/shard_map/while/body/eval_jaxpr/ppermute | solution.py:14
  395.2 4.6 %fusion.96 = (f32[12,8]{1,0:T(8,128)S(1)}, bf16[12,8,2048]{2,1,0:T(8,128)(2,1)S(1)}) fusion(f32[2048]{0:T(1024)S(1)} %fusion.94, bf16[8,12,128]{2,0,1:T(8,128)(2,1)S(1)} %multiply_convert_fusion.5, bf16[2048,12,128]{2,0,1:T(8,128)(2,1)} %get-tuple-element.783), kind=kOutput, calls=%fused_computation.81.clone.1 | convolution fusion | flops 50921376 | bytes 6717824 | tf_op jit(solution)/shard_map/while/body/eval_jaxpr/qhd,khd->hqk/dot_general | solution.py:79
  400.8 3.7 convolution_bitcast_fusion.8
  407.8 5.0 %collective-permute-done = bf16[8,1536]{1,0:T(8,128)(2,1)S(1)} collective-permute-done((bf16[8,1536]{1,0:T(8,128)(2,1)S(1)}, bf16[8,1536]{1,0:T(8,128)(2,1)S(1)}, u32[]{:S(2)}, u32[]{:S(2)}) %collective-permute-start) | collective-permute-done | bytes 24608 | tf_op jit(solution)/shard_map/while/body/eval_jaxpr/ppermute | solution.py:14
  (396 shorter events, 73.1 us)
Async XLA Ops:
  6.5 132.4 %all-gather.2.cloned.1.call-start = ((), (), s32[]{:S(2)}) async-start(), calls=%async_computation | async-start | bytes 12779520 | tf_op jit(solution)/shard_map/all_gather | solution.py:54
  176.4 8.8 %copy-start = (bf16[1,12,128,128]{3,2,1,0:T(8,128)(2,1)S(1)}, bf16[1,12,128,128]{3,2,1,0:T(8,128)(2,1)}, u32[]{:S(2)}) copy-start(bf16[1,12,128,128]{3,2,1,0:T(8,128)(2,1)} %param.14) | copy-start | bytes 1179652
  176.4 8.8 %copy-start.1 = (bf16[1,12,128,128]{3,2,1,0:T(8,128)(2,1)S(1)}, bf16[1,12,128,128]{3,2,1,0:T(8,128)(2,1)}, u32[]{:S(2)}) copy-start(bf16[1,12,128,128]{3,2,1,0:T(8,128)(2,1)} %param.13) | copy-start | bytes 1179652
  176.4 8.8 %copy-start.2 = (bf16[1,12,128,128]{3,2,1,0:T(8,128)(2,1)S(1)}, bf16[1,12,128,128]{3,2,1,0:T(8,128)(2,1)}, u32[]{:S(2)}) copy-start(bf16[1,12,128,128]{3,2,1,0:T(8,128)(2,1)} %param.15) | copy-start | bytes 1179652
  176.4 8.8 %copy-start.3 = (bf16[32,1536]{1,0:T(8,128)(2,1)S(1)}, bf16[32,1536]{1,0:T(8,128)(2,1)}, u32[]{:S(2)}) copy-start(bf16[32,1536]{1,0:T(8,128)(2,1)} %param.10) | copy-start | bytes 294916
  176.4 8.8 %copy-start.4 = (bf16[1,12,128,128]{3,2,1,0:T(8,128)(2,1)S(1)}, bf16[1,12,128,128]{3,2,1,0:T(8,128)(2,1)}, u32[]{:S(2)}) copy-start(bf16[1,12,128,128]{3,2,1,0:T(8,128)(2,1)} %param.12) | copy-start | bytes 1179652
  176.4 8.8 %copy-start.6 = (s32[32]{0:T(128)S(1)}, s32[32]{0:T(128)}, u32[]{:S(2)}) copy-start(s32[32]{0:T(128)} %param.17) | copy-start | bytes 388
  176.5 8.8 %copy-start.7 = (f32[1,12]{1,0:T(1,128)S(1)}, f32[1,12]{1,0:T(1,128)}, u32[]{:S(2)}) copy-start(f32[1,12]{1,0:T(1,128)} %param.16) | copy-start | bytes 148
  198.2 7.8 %collective-permute-start = (bf16[8,1536]{1,0:T(8,128)(2,1)S(1)}, bf16[8,1536]{1,0:T(8,128)(2,1)S(1)}, u32[]{:S(2)}, u32[]{:S(2)}) collective-permute-start(bf16[8,1536]{1,0:T(8,128)(2,1)S(1)} %fusion.101), channel_id=1, source_target_pairs={{0,64},{64,128},{128,192},{192,256},{256,320},{320,384},{384,448},... | collective-permute-start | bytes 73736 | tf_op jit(solution)/shard_map/while/body/eval_jaxpr/ppermute | solution.py:14
  218.9 7.8 %collective-permute-start = (bf16[8,1536]{1,0:T(8,128)(2,1)S(1)}, bf16[8,1536]{1,0:T(8,128)(2,1)S(1)}, u32[]{:S(2)}, u32[]{:S(2)}) collective-permute-start(bf16[8,1536]{1,0:T(8,128)(2,1)S(1)} %fusion.101), channel_id=1, source_target_pairs={{0,64},{64,128},{128,192},{192,256},{256,320},{320,384},{384,448},... | collective-permute-start | bytes 73736 | tf_op jit(solution)/shard_map/while/body/eval_jaxpr/ppermute | solution.py:14
  239.5 7.8 %collective-permute-start = (bf16[8,1536]{1,0:T(8,128)(2,1)S(1)}, bf16[8,1536]{1,0:T(8,128)(2,1)S(1)}, u32[]{:S(2)}, u32[]{:S(2)}) collective-permute-start(bf16[8,1536]{1,0:T(8,128)(2,1)S(1)} %fusion.101), channel_id=1, source_target_pairs={{0,64},{64,128},{128,192},{192,256},{256,320},{320,384},{384,448},... | collective-permute-start | bytes 73736 | tf_op jit(solution)/shard_map/while/body/eval_jaxpr/ppermute | solution.py:14
  260.2 7.8 %collective-permute-start = (bf16[8,1536]{1,0:T(8,128)(2,1)S(1)}, bf16[8,1536]{1,0:T(8,128)(2,1)S(1)}, u32[]{:S(2)}, u32[]{:S(2)}) collective-permute-start(bf16[8,1536]{1,0:T(8,128)(2,1)S(1)} %fusion.101), channel_id=1, source_target_pairs={{0,64},{64,128},{128,192},{192,256},{256,320},{320,384},{384,448},... | collective-permute-start | bytes 73736 | tf_op jit(solution)/shard_map/while/body/eval_jaxpr/ppermute | solution.py:14
  280.9 7.8 %collective-permute-start = (bf16[8,1536]{1,0:T(8,128)(2,1)S(1)}, bf16[8,1536]{1,0:T(8,128)(2,1)S(1)}, u32[]{:S(2)}, u32[]{:S(2)}) collective-permute-start(bf16[8,1536]{1,0:T(8,128)(2,1)S(1)} %fusion.101), channel_id=1, source_target_pairs={{0,64},{64,128},{128,192},{192,256},{256,320},{320,384},{384,448},... | collective-permute-start | bytes 73736 | tf_op jit(solution)/shard_map/while/body/eval_jaxpr/ppermute | solution.py:14
  301.6 7.8 %collective-permute-start = (bf16[8,1536]{1,0:T(8,128)(2,1)S(1)}, bf16[8,1536]{1,0:T(8,128)(2,1)S(1)}, u32[]{:S(2)}, u32[]{:S(2)}) collective-permute-start(bf16[8,1536]{1,0:T(8,128)(2,1)S(1)} %fusion.101), channel_id=1, source_target_pairs={{0,64},{64,128},{128,192},{192,256},{256,320},{320,384},{384,448},... | collective-permute-start | bytes 73736 | tf_op jit(solution)/shard_map/while/body/eval_jaxpr/ppermute | solution.py:14
  322.3 7.8 %collective-permute-start = (bf16[8,1536]{1,0:T(8,128)(2,1)S(1)}, bf16[8,1536]{1,0:T(8,128)(2,1)S(1)}, u32[]{:S(2)}, u32[]{:S(2)}) collective-permute-start(bf16[8,1536]{1,0:T(8,128)(2,1)S(1)} %fusion.101), channel_id=1, source_target_pairs={{0,64},{64,128},{128,192},{192,256},{256,320},{320,384},{384,448},... | collective-permute-start | bytes 73736 | tf_op jit(solution)/shard_map/while/body/eval_jaxpr/ppermute | solution.py:14
  342.9 7.8 %collective-permute-start = (bf16[8,1536]{1,0:T(8,128)(2,1)S(1)}, bf16[8,1536]{1,0:T(8,128)(2,1)S(1)}, u32[]{:S(2)}, u32[]{:S(2)}) collective-permute-start(bf16[8,1536]{1,0:T(8,128)(2,1)S(1)} %fusion.101), channel_id=1, source_target_pairs={{0,64},{64,128},{128,192},{192,256},{256,320},{320,384},{384,448},... | collective-permute-start | bytes 73736 | tf_op jit(solution)/shard_map/while/body/eval_jaxpr/ppermute | solution.py:14
  363.6 7.8 %collective-permute-start = (bf16[8,1536]{1,0:T(8,128)(2,1)S(1)}, bf16[8,1536]{1,0:T(8,128)(2,1)S(1)}, u32[]{:S(2)}, u32[]{:S(2)}) collective-permute-start(bf16[8,1536]{1,0:T(8,128)(2,1)S(1)} %fusion.101), channel_id=1, source_target_pairs={{0,64},{64,128},{128,192},{192,256},{256,320},{320,384},{384,448},... | collective-permute-start | bytes 73736 | tf_op jit(solution)/shard_map/while/body/eval_jaxpr/ppermute | solution.py:14
  384.3 7.8 %collective-permute-start = (bf16[8,1536]{1,0:T(8,128)(2,1)S(1)}, bf16[8,1536]{1,0:T(8,128)(2,1)S(1)}, u32[]{:S(2)}, u32[]{:S(2)}) collective-permute-start(bf16[8,1536]{1,0:T(8,128)(2,1)S(1)} %fusion.101), channel_id=1, source_target_pairs={{0,64},{64,128},{128,192},{192,256},{256,320},{320,384},{384,448},... | collective-permute-start | bytes 73736 | tf_op jit(solution)/shard_map/while/body/eval_jaxpr/ppermute | solution.py:14
  405.0 7.8 %collective-permute-start = (bf16[8,1536]{1,0:T(8,128)(2,1)S(1)}, bf16[8,1536]{1,0:T(8,128)(2,1)S(1)}, u32[]{:S(2)}, u32[]{:S(2)}) collective-permute-start(bf16[8,1536]{1,0:T(8,128)(2,1)S(1)} %fusion.101), channel_id=1, source_target_pairs={{0,64},{64,128},{128,192},{192,256},{256,320},{320,384},{384,448},... | collective-permute-start | bytes 73736 | tf_op jit(solution)/shard_map/while/body/eval_jaxpr/ppermute | solution.py:14
  412.8 0.6 copy-start.5
Sparse Core Ops, SparseCore 0:
  12.4 126.4 all-gather.1
where the time goes:
time: 422 us; the launch traced here: 420 us
  waiting for transfers between devices  178 us (42%)
  matrix products  115 us (27%)
  local copies, waits for them, and re-layouts  79.1 us (19%)
  starting transfers between devices  22.5 us (5%)
  between operations  13.6 us (3%)
  other arithmetic  10.3 us (2%)
    all_gather x1, waiting for transfers between devices, body(): lax.all_gather(key_pair(stale_normed, key_weight, value_weight), 'ctx', a...  124 us
    ppermute x11, waiting for transfers between devices, from_behind(): return lax.ppermute(array, axis, pairs)  53.8 us
    dot_general x11, matrix products, advance(): jnp.einsum('qhd,khd->hqk', queries, far_keys, preferred_element_type=jnp....  50.6 us
    dot_general x11, matrix products, advance(): jnp.einsum('hqk,khd->qhd', e_far.astype(jnp.bfloat16), far_values, prefer...  40.8 us
    ppermute x11, starting transfers between devices, from_behind(): return lax.ppermute(array, axis, pairs)  22.5 us
    slice x2, local copies, waits for them, and re-layouts, body(): far_values = pairs[1].reshape(total, heads, head_size)  19 us
    unnamed x20, local copies, waits for them, and re-layouts  18.1 us
    dot_general x46, matrix products, project(): jnp.einsum('nhd,hde->nhe', normed.reshape(count, weight.shape[0], weight....  16.2 us
  transfers between devices with their start and end apart: 12, of which 12 were waited for; matrix products, arithmetic and copies ran while one was open for 3% of the time, Pallas kernels for 0%

commit v1 on v0

v1 whole, which is shorter than its diff:
```python
import functools
import math

import jax
import jax.numpy as jnp
from jax import lax
from jax.experimental import pallas as pl
from jax.experimental.pallas import tpu as pltpu
from jax.sharding import PartitionSpec as P

F32 = jnp.float32
BF16 = jnp.bfloat16
MESH = pl.DeviceIdType.MESH
EPS = 1e-6
HD = 128
TILE = 32
QUAD = 4
TOK = QUAD * TILE
GRP = 3
FEAT = QUAD * GRP * HD


def nn(a, b):
    return lax.dot_general(a, b, (((1,), (0,)), ((), ())), preferred_element_type=F32)


def nt(a, b):
    return lax.dot_general(a, b, (((1,), (1,)), ((), ())), preferred_element_type=F32)


def tn(a, b):
    return lax.dot_general(a, b, (((0,), (0,)), ((), ())), preferred_element_type=F32)


def arrived(ref, sem):
    pltpu.make_async_copy(ref, ref, sem).wait()


def kernel(
    sections, nz,
    x_ref, stale_ref, wq_ref, wk_ref, wv_ref, wo_ref, scale_ref, assign_ref,
    out_ref,
    stv, wts, normed, near, mask, xin, wk3, wT, wvoT, keys, vals, ht, ot, ob, sumsq, sumsq_out,
    load_sem, xs_sem, xr_sem, ms_sem, mr_sem, qs_sem, qr_sem, ring_sem, sib_sem, near_sem,
    hs_sem, hr_sem, ss_sem, sr_sem, os_sem, or_sem,
):
    s = lax.axis_index("section")
    c = lax.axis_index("ctx")
    yh = c // (2 * nz)
    z = (c // 2) % nz
    core = c % 2
    half = nz // 2

    def at(section, y, zz, k):
        return (section, (y * nz + zz) * 2 + k)

    def peer(d):
        return (yh + d) % QUAD

    right = at(s, yh, (z + 1) % nz, core)
    left = at(s, yh, (z + nz - 1) % nz, core)
    sibling = at(s, yh, z, 1 - core)
    first = s == 0
    has_next = s < sections - 1
    mine = pl.ds(pl.multiple_of(yh * TILE, TILE), TILE)
    columns = pl.ds(pl.multiple_of(yh * (GRP * HD), GRP * HD), GRP * HD)

    def remote(src, dst, send, recv, device):
        return pltpu.make_async_remote_copy(
            src_ref=src, dst_ref=dst, send_sem=send, recv_sem=recv,
            device_id=device, device_id_type=MESH,
        )

    load_stale = pltpu.make_async_copy(stale_ref.at[0], stv, load_sem.at[0])
    load_stale.start()
    loads = []
    for i, w in enumerate((wk_ref, wq_ref, wv_ref, wo_ref)):
        loads.append(
            pltpu.make_async_copy(w.at[0, pl.ds(yh * GRP, GRP)], wts.at[i], load_sem.at[i + 1])
        )
        loads[-1].start()
    load_x = pltpu.make_async_copy(x_ref.at[:, columns], xin.at[mine, :], load_sem.at[5])

    @pl.when(first)
    def _():
        load_x.start()

    barrier = pltpu.get_barrier_semaphore()

    def greet(device):
        pl.semaphore_signal(barrier, inc=1, device_id=device, device_id_type=MESH)

    for d in range(1, QUAD):
        greet(at(s, peer(d), z, core))
    for device in (right, left, sibling):
        greet(device)

    @pl.when(has_next)
    def _():
        for d in range(QUAD):
            greet(at(s + 1, peer(d), z, core))

    @pl.when(s > 0)
    def _():
        for d in range(QUAD):
            greet(at(s - 1, peer(d), z, core))

    load_stale.wait()
    st = stv[...].astype(F32)
    n = (st * lax.rsqrt(jnp.mean(st * st, axis=-1, keepdims=True) + EPS)).astype(BF16)
    for h in range(QUAD * GRP):
        normed[h] = n[:, h * HD:(h + 1) * HD]
    near[0, 0, :, mine, :] = normed[pl.ds(yh * GRP, GRP)]

    row = assign_ref[...].astype(F32)
    row = jnp.concatenate([row] * QUAD, axis=1)
    lane = lax.broadcasted_iota(jnp.int32, (TILE, TOK), 1)
    sub = lax.broadcasted_iota(jnp.int32, (TILE, TOK), 0)
    rows = jnp.broadcast_to(row, (TILE, TOK))
    col = jnp.sum(jnp.where(lane == sub, rows, 0.0), axis=1, keepdims=True)
    fresh = jnp.where(col <= rows, 1.0, 0.0) * jnp.where(lane // TILE == yh, 1.0, 0.0)
    mask[mine, :] = fresh.astype(BF16)

    pl.semaphore_wait(
        barrier, 6 + QUAD * jnp.where(has_next, 1, 0) + QUAD * jnp.where(s > 0, 1, 0)
    )

    quad_sends, mask_sends, x_sends = [], [], []
    for d in range(1, QUAD):
        to = at(s, peer(d), z, core)
        quad_sends.append(remote(
            normed.at[pl.ds(peer(d) * GRP, GRP)], near.at[0, 0, :, mine, :],
            qs_sem.at[d - 1], qr_sem.at[d - 1], to,
        ))
        mask_sends.append(remote(
            mask.at[mine, :], mask.at[mine, :], ms_sem.at[d - 1], mr_sem.at[d - 1], to,
        ))
        x_sends.append(remote(
            x_ref.at[:, pl.ds(pl.multiple_of(peer(d) * (GRP * HD), GRP * HD), GRP * HD)],
            xin.at[mine, :], xs_sem.at[d - 1], xr_sem.at[d - 1], to,
        ))
    for copy in quad_sends:
        copy.start()

    @pl.when(first)
    def _():
        for copy in x_sends:
            copy.start()

    for copy in mask_sends:
        copy.start()

    for copy in loads:
        copy.wait()
    for h in range(GRP):
        wk = wts[0, h]
        wk3[h] = wk
        wvo = nn(wts[2, h], wts[3, h]).T.astype(BF16)
        wvoT[h] = wvo
        wT[h, 0:HD, :] = wts[1, h].astype(F32).T.astype(BF16)
        wT[h, HD:2 * HD, :] = wk.astype(F32).T.astype(BF16)
        wT[h, 2 * HD:, :] = wvo

    def to_right(t, h):
        return remote(
            near.at[(nz - t) % nz, 0, h], near.at[nz - t - 1, 0, h],
            ring_sem.at[0, t, h], near_sem.at[nz - t - 1, 0, h], right,
        )

    def to_left(t, h):
        return remote(
            near.at[t, 0, h], near.at[t + 1, 0, h],
            ring_sem.at[1, t, h], near_sem.at[t + 1, 0, h], left,
        )

    def to_sibling(r, h):
        return remote(
            near.at[r, 0, h], near.at[r, 1, h],
            sib_sem.at[r, h], near_sem.at[r, 1, h], sibling,
        )

    sends = []

    def start(copy):
        copy.start()
        sends.append(copy)

    def prepare(r, k):
        for h in range(GRP):
            block = near[r, k, h]
            raw = nn(block, wk3[h])
            scaled = raw * lax.rsqrt(jnp.mean(raw * raw, axis=-1, keepdims=True) + EPS)
            keys[h, r * TOK:(r + 1) * TOK, k * HD:(k + 1) * HD] = scaled.astype(BF16)
            vals[h, k * HD:(k + 1) * HD, r * TOK:(r + 1) * TOK] = nt(wvoT[h], block).astype(BF16)

    def sibling_slots(slots):
        for r in slots:
            for h in range(GRP):
                arrived(near.at[r, 1, h], near_sem.at[r, 1, h])
            prepare(r, 1)

    for d in range(1, QUAD):
        source = pl.ds(pl.multiple_of(((yh + QUAD - d) % QUAD) * TILE, TILE), TILE)
        arrived(near.at[0, 0, :, source, :], qr_sem.at[d - 1])
    for h in range(GRP):
        if half > 1 or h < 2:
            start(to_right(0, h))
        if half > 1 or h == 2:
            start(to_left(0, h))
        start(to_sibling(0, h))
    prepare(0, 0)
    before = [0]
    for t in range(1, half + 1):
        back = nz - t
        for h in range(GRP):
            arrived(near.at[back, 0, h], near_sem.at[back, 0, h])
            if t < half - 1 or (t == half - 1 and h < 2):
                start(to_right(t, h))
            start(to_sibling(back, h))
            if back != t:
                arrived(near.at[t, 0, h], near_sem.at[t, 0, h])
                if t < half - 1 or (t == half - 1 and h == 2):
                    start(to_left(t, h))
                start(to_sibling(t, h))
        sibling_slots(before)
        before = [back] if back == t else [back, t]
        for r in before:
            prepare(r, 0)
    sibling_slots(before)

    for d in range(1, QUAD):
        source = pl.ds(pl.multiple_of(((yh + QUAD - d) % QUAD) * TILE, TILE), TILE)
        arrived(mask.at[source, :], mr_sem.at[d - 1])

    def sum_to(section, d):
        return remote(
            sumsq_out, sumsq.at[d], ss_sem.at[d], sr_sem.at[d], at(section, peer(d), z, core)
        )

    def squares(values):
        return jnp.sum((values * values).reshape(HD // 8, 8, TOK), axis=0)

    @pl.when(first)
    def _():
        load_x.wait()
        for d in range(1, QUAD):
            source = pl.ds(pl.multiple_of(((yh + QUAD - d) % QUAD) * TILE, TILE), TILE)
            arrived(xin.at[source, :], xr_sem.at[d - 1])
        part = jnp.zeros((8, TOK), F32)
        for h in range(GRP):
            turned = xin[:, h * HD:(h + 1) * HD].astype(F32).T
            ht[h] = turned.astype(BF16)
            part = part + squares(turned)
        sumsq_out[...] = part
        sumsq[0] = part
        own = [sum_to(s, d) for d in range(1, QUAD)]
        for copy in own:
            copy.start()
        for copy in own:
            copy.wait_send()

    @pl.when(s > 0)
    def _():
        for h in range(GRP):
            arrived(ht.at[h], hr_sem.at[h])
        arrived(sumsq.at[0], sr_sem.at[0])

    for d in range(1, QUAD):
        arrived(sumsq.at[d], sr_sem.at[d])

    total = sumsq[0] + sumsq[1] + sumsq[2] + sumsq[3]
    mean_sq = jnp.sum(total, axis=0, keepdims=True) * (1.0 / FEAT) + EPS
    inv = lax.rsqrt(mean_sq)
    eps = EPS * mean_sq
    chosen = mask[...].astype(F32)
    keep = jnp.concatenate([1.0 - chosen, jnp.ones_like(chosen)], axis=1)
    zero = jnp.zeros((HD, TOK), BF16)

    def hand_on(h):
        return remote(ot.at[h], ht.at[h], hs_sem.at[h], hr_sem.at[h], at(s + 1, yh, z, core))

    part = jnp.zeros((8, TOK), F32)
    for h in range(GRP):
        hidden = ht[h]
        mapped = nn(wT[h], hidden)
        pq, pk, pv = mapped[0:HD], mapped[HD:2 * HD], mapped[2 * HD:]
        scale = scale_ref[0, yh * GRP + h] * (math.log2(math.e) / math.sqrt(HD))
        aq = lax.rsqrt(jnp.sum(pq * pq, axis=0, keepdims=True) * (1.0 / HD) + eps) * scale
        bk = lax.rsqrt(jnp.sum(pk * pk, axis=0, keepdims=True) * (1.0 / HD) + eps)
        q = (pq * aq).astype(BF16)
        kf = (pk * bk).astype(BF16)
        vf = (pv * inv).astype(BF16)
        pair = jnp.concatenate(
            [jnp.concatenate([q, zero], axis=1), jnp.concatenate([zero, q], axis=1)], axis=0
        )
        e = jnp.exp2(nn(keys[h], pair))
        e = jnp.concatenate([e[0:TOK] * keep, e[TOK:]], axis=0)
        e_new = jnp.exp2(tn(kf, q)) * chosen
        den = jnp.sum(e.reshape(nz * TOK // 8, 8, 2 * TOK), axis=0)
        den = den[:, :TOK] + den[:, TOK:] + jnp.sum(e_new.reshape(TOK // 8, 8, TOK), axis=0)
        den = jnp.sum(den, axis=0, keepdims=True)
        both = nn(vals[h], e.astype(BF16))
        numer = both[0:HD, 0:TOK] + both[HD:, TOK:] + nn(vf, e_new.astype(BF16))
        result = (hidden.astype(F32) + numer * (1.0 / den)).astype(BF16)
        ot[h] = result

        @pl.when(has_next)
        def _():
            hand_on(h).start()

        part = part + squares(result.astype(F32))

    @pl.when(has_next)
    def _():
        sumsq_out[...] = part
        for d in range(QUAD):
            sum_to(s + 1, d).start()

    for h in range(GRP):
        ob[:, h * HD:(h + 1) * HD] = ot[h].astype(F32).T.astype(BF16)
    own_out = pltpu.make_async_copy(ob.at[mine, :], out_ref.at[0, :, columns], load_sem.at[0])
    own_out.start()
    outs = []
    for d in range(1, QUAD):
        theirs = pl.ds(pl.multiple_of(peer(d) * TILE, TILE), TILE)
        outs.append(remote(
            ob.at[theirs, :], out_ref.at[0, :, columns],
            os_sem.at[d - 1], or_sem.at[d - 1], at(s, peer(d), z, core),
        ))
        outs[-1].start()

    for copy in sends + quad_sends + mask_sends:
        copy.wait_send()

    @pl.when(first)
    def _():
        for copy in x_sends:
            copy.wait_send()

    @pl.when(has_next)
    def _():
        for h in range(GRP):
            hand_on(h).wait_send()
        for d in range(QUAD):
            sum_to(s + 1, d).wait_send()

    own_out.wait()
    for d, copy in enumerate(outs, 1):
        copy.wait_send()
        theirs = pl.ds(
            pl.multiple_of(((yh + QUAD - d) % QUAD) * (GRP * HD), GRP * HD), GRP * HD
        )
        arrived(out_ref.at[0, :, theirs], or_sem.at[d - 1])


def solution(mesh):
    sections = mesh.shape["section"]
    nz = mesh.shape["ctx"] // (2 * QUAD)
    keys = nz * TOK

    def body(x_in, stale_inputs, w_query, w_key, w_value, w_out, score_scale, assign):
        anywhere = pl.BlockSpec(memory_space=pl.ANY)
        dma = pltpu.SemaphoreType.DMA
        return pl.pallas_call(
            functools.partial(kernel, sections, nz),
            out_shape=jax.ShapeDtypeStruct(stale_inputs.shape, BF16),
            in_specs=[anywhere] * 6 + [
                pl.BlockSpec(memory_space=pltpu.SMEM),
                pl.BlockSpec(memory_space=pltpu.VMEM),
            ],
            out_specs=anywhere,
            scratch_shapes=[
                pltpu.VMEM((TILE, FEAT), BF16),
                pltpu.VMEM((4, GRP, HD, HD), BF16),
                pltpu.VMEM((QUAD * GRP, TILE, HD), BF16),
                pltpu.VMEM((nz, 2, GRP, TOK, HD), BF16),
                pltpu.VMEM((TOK, TOK), BF16),
                pltpu.VMEM((TOK, GRP * HD), BF16),
                pltpu.VMEM((GRP, HD, HD), BF16),
                pltpu.VMEM((GRP, 3 * HD, HD), BF16),
                pltpu.VMEM((GRP, HD, HD), BF16),
                pltpu.VMEM((GRP, keys, 2 * HD), BF16),
                pltpu.VMEM((GRP, 2 * HD, keys), BF16),
                pltpu.VMEM((GRP, HD, TOK), BF16),
                pltpu.VMEM((GRP, HD, TOK), BF16),
                pltpu.VMEM((TOK, GRP * HD), BF16),
                pltpu.VMEM((QUAD, 8, TOK), F32),
                pltpu.VMEM((8, TOK), F32),
                dma((6,)),
                dma((3,)), dma((3,)),
                dma((3,)), dma((3,)),
                dma((3,)), dma((3,)),
                dma((2, nz // 2, GRP)),
                dma((nz, GRP)),
                dma((nz, 2, GRP)),
                dma((GRP,)), dma((GRP,)),
                dma((QUAD,)), dma((QUAD,)),
                dma((3,)), dma((3,)),
            ],
            compiler_params=pltpu.CompilerParams(
                collective_id=0, has_side_effects=True, vmem_limit_bytes=40 * 2**20
            ),
            name="relay",
        )(
            x_in, stale_inputs, w_query, w_key, w_value, w_out, score_scale,
            assign.reshape(1, TILE),
        )

    return jax.shard_map(
        body,
        mesh=mesh,
        in_specs=(
            P("ctx", None),
            P("section", "ctx", None),
            P("section", None, None, None),
            P("section", None, None, None),
            P("section", None, None, None),
            P("section", None, None, None),
            P("section", None),
            P("ctx"),
        ),
        out_specs=P("section", "ctx", None),
        check_vma=False,
    )
```

time: 422 us -> 108 us (0.26)
  the two profiles are of different devices: /device:TPU:8 before, /device:TPU:14 now
where the time goes in v1:
time: 108 us; the launch traced here: 107 us
  Pallas kernels  100 us (93%)
  local copies, waits for them, and re-layouts  7.08 us (7%)
    pallas_call x1, Pallas kernels, body(): pl.pallas_call(functools.partial(kernel, sections, nz), out_shape=jax.Sha...  100 us
    unnamed x17, local copies, waits for them, and re-layouts  7.08 us

profile of v1, /device:TPU:14, one launch (start us, length us, event | category | flops | bytes accessed | tf_op | source)
XLA Modules:
  0.0 107.3 jit_solution(14364995870457778262)
XLA Ops:
  0.0 0.0 copy-start.7
  0.0 0.0 copy-start.6
  0.0 0.7 copy-done.7
  0.7 0.0 copy-done.6
  0.7 0.0 copy-start
  0.7 1.0 copy-done
  1.7 0.0 copy-start.1
  1.7 1.0 copy-done.1
  2.7 0.0 copy-start.2
  2.7 1.0 copy-done.2
  3.7 0.0 copy-start.3
  3.7 1.0 copy-done.3
  4.7 0.0 copy-start.4
  4.7 0.9 copy-done.4
  5.6 0.0 copy-start.5
  5.6 0.9 copy-done.5
  6.4 100.2 %relay.1 = bf16[1,32,1536]{2,1,0:T(8,128)(2,1)S(1)} custom-call(bf16[32,1536]{1,0:T(8,128)(2,1)S(1)} %copy-done.4, bf16[1,32,1536]{2,1,0:T(8,128)(2,1)S(1)} %copy-done.5, bf16[1,12,128,128]{3,2,1,0:T(8,128)(2,1)S(1)} %copy-done, bf16[1,12,128,128]{3,2,1,0:T(8,128)(2,1)S(1)} %copy-done.1, bf16[1,12,128,128]{3,2,1,0:T(8,128)(2,1)S(1)} %copy-done.2, ...), custom_call_target="tpu_custom_call" | custom-call | tf_op jit(solution)/shard_map/relay/pallas_call | solution.py:364
  106.7 0.6 copy.10
Async XLA Ops:
  0.0 0.7 copy-start.7
  0.0 0.7 copy-start.6
  0.7 1.0 copy-start
  1.7 1.0 copy-start.1
  2.7 1.0 copy-start.2
  3.7 1.0 copy-start.3
  4.7 0.9 copy-start.4
  5.6 0.9 copy-start.5

commit v2 on v1

--- a/solution.py
+++ b/solution.py
@@ -40,7 +40,7 @@
     sections, nz,
     x_ref, stale_ref, wq_ref, wk_ref, wv_ref, wo_ref, scale_ref, assign_ref,
     out_ref,
-    stv, wts, normed, near, mask, xin, wk3, wT, wvoT, keys, vals, ht, ot, ob, sumsq, sumsq_out,
+    stv, wts, normed, near, mask, xin, wk3, wT, wvoT, keys, vals, ht, ot, ob, sumsq, sumsq_out, mapped, raw,
     load_sem, xs_sem, xr_sem, ms_sem, mr_sem, qs_sem, qr_sem, ring_sem, sib_sem, near_sem,
     hs_sem, hr_sem, ss_sem, sr_sem, os_sem, or_sem,
 ):
@@ -208,6 +208,33 @@
         if half > 1 or h == 2:
             start(to_left(0, h))
         start(to_sibling(0, h))
+    def sum_to(section, d):
+        return remote(
+            sumsq_out, sumsq.at[d], ss_sem.at[d], sr_sem.at[d], at(section, peer(d), z, core)
+        )
+
+    def squares(values):
+        return jnp.sum((values * values).reshape(HD // 8, 8, TOK), axis=0)
+
+    @pl.when(first)
+    def _():
+        load_x.wait()
+        for d in range(1, QUAD):
+            source = pl.ds(pl.multiple_of(((yh + QUAD - d) % QUAD) * TILE, TILE), TILE)
+            arrived(xin.at[source, :], xr_sem.at[d - 1])
+        part = jnp.zeros((8, TOK), F32)
+        for h in range(GRP):
+            turned = xin[:, h * HD:(h + 1) * HD].astype(F32).T
+            ht[h] = turned.astype(BF16)
+            part = part + squares(turned)
+        sumsq_out[...] = part
+        sumsq[0] = part
+        own = [sum_to(s, d) for d in range(1, QUAD)]
+        for copy in own:
+            copy.start()
+        for copy in own:
+            copy.wait_send()
+
     prepare(0, 0)
     before = [0]
     for t in range(1, half + 1):
@@ -232,37 +259,24 @@
         source = pl.ds(pl.multiple_of(((yh + QUAD - d) % QUAD) * TILE, TILE), TILE)
         arrived(mask.at[source, :], mr_sem.at[d - 1])
 
-    def sum_to(section, d):
-        return remote(
-            sumsq_out, sumsq.at[d], ss_sem.at[d], sr_sem.at[d], at(section, peer(d), z, core)
-        )
-
-    def squares(values):
-        return jnp.sum((values * values).reshape(HD // 8, 8, TOK), axis=0)
-
-    @pl.when(first)
-    def _():
-        load_x.wait()
-        for d in range(1, QUAD):
-            source = pl.ds(pl.multiple_of(((yh + QUAD - d) % QUAD) * TILE, TILE), TILE)
-            arrived(xin.at[source, :], xr_sem.at[d - 1])
-        part = jnp.zeros((8, TOK), F32)
-        for h in range(GRP):
-            turned = xin[:, h * HD:(h + 1) * HD].astype(F32).T
-            ht[h] = turned.astype(BF16)
-            part = part + squares(turned)
-        sumsq_out[...] = part
-        sumsq[0] = part
-        own = [sum_to(s, d) for d in range(1, QUAD)]
-        for copy in own:
-            copy.start()
-        for copy in own:
-            copy.wait_send()
+    chosen = mask[...].astype(F32)
+    keep = jnp.concatenate([1.0 - chosen, jnp.ones_like(chosen)], axis=1)
+    zero = jnp.zeros((HD, TOK), BF16)
+    for h in range(GRP):
+        @pl.when(s > 0)
+        def _():
+            arrived(ht.at[h], hr_sem.at[h])
+
+        both = nn(wT[h], ht[h])
+        mapped[h] = both
+        p = both[0:HD].astype(BF16)
+        pair = jnp.concatenate(
+            [jnp.concatenate([p, zero], axis=1), jnp.concatenate([zero, p], axis=1)], axis=0
+        )
+        raw[h] = nn(keys[h], pair)
 
     @pl.when(s > 0)
     def _():
-        for h in range(GRP):
-            arrived(ht.at[h], hr_sem.at[h])
         arrived(sumsq.at[0], sr_sem.at[0])
 
     for d in range(1, QUAD):
@@ -272,9 +286,6 @@
     mean_sq = jnp.sum(total, axis=0, keepdims=True) * (1.0 / FEAT) + EPS
     inv = lax.rsqrt(mean_sq)
     eps = EPS * mean_sq
-    chosen = mask[...].astype(F32)
-    keep = jnp.concatenate([1.0 - chosen, jnp.ones_like(chosen)], axis=1)
-    zero = jnp.zeros((HD, TOK), BF16)
 
     def hand_on(h):
         return remote(ot.at[h], ht.at[h], hs_sem.at[h], hr_sem.at[h], at(s + 1, yh, z, core))
@@ -282,18 +293,14 @@
     part = jnp.zeros((8, TOK), F32)
     for h in range(GRP):
         hidden = ht[h]
-        mapped = nn(wT[h], hidden)
-        pq, pk, pv = mapped[0:HD], mapped[HD:2 * HD], mapped[2 * HD:]
+        pq, pk, pv = mapped[h, 0:HD], mapped[h, HD:2 * HD], mapped[h, 2 * HD:]
         scale = scale_ref[0, yh * GRP + h] * (math.log2(math.e) / math.sqrt(HD))
         aq = lax.rsqrt(jnp.sum(pq * pq, axis=0, keepdims=True) * (1.0 / HD) + eps) * scale
         bk = lax.rsqrt(jnp.sum(pk * pk, axis=0, keepdims=True) * (1.0 / HD) + eps)
         q = (pq * aq).astype(BF16)
         kf = (pk * bk).astype(BF16)
         vf = (pv * inv).astype(BF16)
-        pair = jnp.concatenate(
-            [jnp.concatenate([q, zero], axis=1), jnp.concatenate([zero, q], axis=1)], axis=0
-        )
-        e = jnp.exp2(nn(keys[h], pair))
+        e = jnp.exp2(raw[h] * jnp.concatenate([aq, aq], axis=1))
         e = jnp.concatenate([e[0:TOK] * keep, e[TOK:]], axis=0)
         e_new = jnp.exp2(tn(kf, q)) * chosen
         den = jnp.sum(e.reshape(nz * TOK // 8, 8, 2 * TOK), axis=0)
@@ -313,7 +320,7 @@
     @pl.when(has_next)
     def _():
         sumsq_out[...] = part
-        for d in range(QUAD):
+        for d in (2, 1, 3, 0):
             sum_to(s + 1, d).start()
 
     for h in range(GRP):
@@ -386,6 +393,8 @@
                 pltpu.VMEM((TOK, GRP * HD), BF16),
                 pltpu.VMEM((QUAD, 8, TOK), F32),
                 pltpu.VMEM((8, TOK), F32),
+                pltpu.VMEM((GRP, 3 * HD, TOK), F32),
+                pltpu.VMEM((GRP, keys, 2 * TOK), F32),
                 dma((6,)),
                 dma((3,)), dma((3,)),
                 dma((3,)), dma((3,)),
@@ -398,7 +407,7 @@
                 dma((3,)), dma((3,)),
             ],
             compiler_params=pltpu.CompilerParams(
-                collective_id=0, has_side_effects=True, vmem_limit_bytes=40 * 2**20
+                collective_id=0, has_side_effects=True, vmem_limit_bytes=60 * 2**20
             ),
             name="relay",
         )(

time: 108 us -> 92 us (0.85)
  Pallas kernels: 100 us -> 90.3 us
  local copies, waits for them, and re-layouts: 7.08 us -> 1.54 us
    pallas_call x1, Pallas kernels: 100 us -> 90.3 us  [body(): pl.pallas_call(functools.partial(kernel, sections, nz), out_shape=jax.Sha...]
    unnamed x17 -> x1, local copies, waits for them, and re-layouts: 7.08 us -> 1.54 us
where the time goes in v2:
time: 92 us; the launch traced here: 91.8 us
  Pallas kernels  90.3 us (98%)
  local copies, waits for them, and re-layouts  1.54 us (2%)
    pallas_call x1, Pallas kernels, body(): pl.pallas_call(functools.partial(kernel, sections, nz), out_shape=jax.Sha...  90.3 us

profile of v2, /device:TPU:14, one launch (start us, length us, event | category | flops | bytes accessed | tf_op | source)
XLA Modules:
  0.0 91.8 jit_solution(16496792882603340051)
XLA Ops:
  0.0 90.3 %relay.1 = bf16[1,32,1536]{2,1,0:T(8,128)(2,1)} custom-call(bf16[32,1536]{1,0:T(8,128)(2,1)} %x_ref.1, bf16[1,32,1536]{2,1,0:T(8,128)(2,1)} %stale_ref.1, bf16[1,12,128,128]{3,2,1,0:T(8,128)(2,1)} %wq_ref.1, bf16[1,12,128,128]{3,2,1,0:T(8,128)(2,1)} %wk_ref.1, bf16[1,12,128,128]{3,2,1,0:T(8,128)(2,1)} %wv_ref.1, bf16[1,12,128,128]{3,2,1,0:T(8,128)(2,1)} %wo_ref.1, ...), custom_call_target="tpu_custom_call" | custom-call | tf_op jit(solution)/shard_map/relay/pallas_call | solution.py:371
  90.3 1.5 %copy.10 = bf16[1,32,1536]{2,1,0:T(8,128)(2,1)} copy(bf16[1,32,1536]{2,1,0:T(8,128)(2,1)} %relay.1) | data formatting | bytes 196608

commit v3 on v2

--- a/solution.py
+++ b/solution.py
@@ -41,7 +41,7 @@
     x_ref, stale_ref, wq_ref, wk_ref, wv_ref, wo_ref, scale_ref, assign_ref,
     out_ref,
     stv, wts, normed, near, mask, xin, wk3, wT, wvoT, keys, vals, ht, ot, ob, sumsq, sumsq_out, mapped, raw,
-    load_sem, xs_sem, xr_sem, ms_sem, mr_sem, qs_sem, qr_sem, ring_sem, sib_sem, near_sem,
+    load_sem, xs_sem, xr_sem, ms_sem, mr_sem, qs_sem, ring_sem, near_sem,
     hs_sem, hr_sem, ss_sem, sr_sem, os_sem, or_sem,
 ):
     s = lax.axis_index("section")
@@ -49,21 +49,27 @@
     yh = c // (2 * nz)
     z = (c // 2) % nz
     core = c % 2
-    half = nz // 2
+    zh = z // 2
+    m = (z % 2) * 2 + core
 
     def at(section, y, zz, k):
         return (section, (y * nz + zz) * 2 + k)
 
     def peer(d):
-        return (yh + d) % QUAD
-
-    right = at(s, yh, (z + 1) % nz, core)
-    left = at(s, yh, (z + nz - 1) % nz, core)
-    sibling = at(s, yh, z, 1 - core)
+        return (m + d) % QUAD
+
+    def mate(section, d):
+        return at(section, yh, 2 * zh + peer(d) // 2, peer(d) % 2)
+
+    def along(axis, step):
+        if axis == 0:
+            return at(s, (yh + QUAD + step) % QUAD, z, core)
+        return at(s, yh, (z + nz + 2 * step) % nz, core)
+
     first = s == 0
     has_next = s < sections - 1
-    mine = pl.ds(pl.multiple_of(yh * TILE, TILE), TILE)
-    columns = pl.ds(pl.multiple_of(yh * (GRP * HD), GRP * HD), GRP * HD)
+    mine = pl.ds(pl.multiple_of(m * TILE, TILE), TILE)
+    columns = pl.ds(pl.multiple_of(m * (GRP * HD), GRP * HD), GRP * HD)
 
     def remote(src, dst, send, recv, device):
         return pltpu.make_async_remote_copy(
@@ -76,7 +82,7 @@
     loads = []
     for i, w in enumerate((wk_ref, wq_ref, wv_ref, wo_ref)):
         loads.append(
-            pltpu.make_async_copy(w.at[0, pl.ds(yh * GRP, GRP)], wts.at[i], load_sem.at[i + 1])
+            pltpu.make_async_copy(w.at[0, pl.ds(m * GRP, GRP)], wts.at[i], load_sem.at[i + 1])
         )
         loads[-1].start()
     load_x = pltpu.make_async_copy(x_ref.at[:, columns], xin.at[mine, :], load_sem.at[5])
@@ -91,26 +97,27 @@
         pl.semaphore_signal(barrier, inc=1, device_id=device, device_id_type=MESH)
 
     for d in range(1, QUAD):
-        greet(at(s, peer(d), z, core))
-    for device in (right, left, sibling):
-        greet(device)
+        greet(mate(s, d))
+    for axis in range(2):
+        greet(along(axis, 1))
+        greet(along(axis, -1))
 
     @pl.when(has_next)
     def _():
         for d in range(QUAD):
-            greet(at(s + 1, peer(d), z, core))
+            greet(mate(s + 1, d))
 
     @pl.when(s > 0)
     def _():
         for d in range(QUAD):
-            greet(at(s - 1, peer(d), z, core))
+            greet(mate(s - 1, d))
 
     load_stale.wait()
     st = stv[...].astype(F32)
     n = (st * lax.rsqrt(jnp.mean(st * st, axis=-1, keepdims=True) + EPS)).astype(BF16)
     for h in range(QUAD * GRP):
         normed[h] = n[:, h * HD:(h + 1) * HD]
-    near[0, 0, :, mine, :] = normed[pl.ds(yh * GRP, GRP)]
+    near[0, 0, m] = normed[pl.ds(m * GRP, GRP)]
 
     row = assign_ref[...].astype(F32)
     row = jnp.concatenate([row] * QUAD, axis=1)
@@ -118,19 +125,19 @@
     sub = lax.broadcasted_iota(jnp.int32, (TILE, TOK), 0)
     rows = jnp.broadcast_to(row, (TILE, TOK))
     col = jnp.sum(jnp.where(lane == sub, rows, 0.0), axis=1, keepdims=True)
-    fresh = jnp.where(col <= rows, 1.0, 0.0) * jnp.where(lane // TILE == yh, 1.0, 0.0)
+    fresh = jnp.where(col <= rows, 1.0, 0.0) * jnp.where(lane // TILE == m, 1.0, 0.0)
     mask[mine, :] = fresh.astype(BF16)
 
     pl.semaphore_wait(
-        barrier, 6 + QUAD * jnp.where(has_next, 1, 0) + QUAD * jnp.where(s > 0, 1, 0)
+        barrier, 7 + QUAD * jnp.where(has_next, 1, 0) + QUAD * jnp.where(s > 0, 1, 0)
     )
 
     quad_sends, mask_sends, x_sends = [], [], []
     for d in range(1, QUAD):
-        to = at(s, peer(d), z, core)
+        to = mate(s, d)
         quad_sends.append(remote(
-            normed.at[pl.ds(peer(d) * GRP, GRP)], near.at[0, 0, :, mine, :],
-            qs_sem.at[d - 1], qr_sem.at[d - 1], to,
+            normed.at[pl.ds(peer(d) * GRP, GRP)], near.at[0, 0, m],
+            qs_sem.at[d - 1], near_sem.at[0, 0, m], to,
         ))
         mask_sends.append(remote(
             mask.at[mine, :], mask.at[mine, :], ms_sem.at[d - 1], mr_sem.at[d - 1], to,
@@ -161,56 +168,53 @@
         wT[h, HD:2 * HD, :] = wk.astype(F32).T.astype(BF16)
         wT[h, 2 * HD:, :] = wvo
 
-    def to_right(t, h):
-        return remote(
-            near.at[(nz - t) % nz, 0, h], near.at[nz - t - 1, 0, h],
-            ring_sem.at[0, t, h], near_sem.at[nz - t - 1, 0, h], right,
-        )
-
-    def to_left(t, h):
-        return remote(
-            near.at[t, 0, h], near.at[t + 1, 0, h],
-            ring_sem.at[1, t, h], near_sem.at[t + 1, 0, h], left,
-        )
-
-    def to_sibling(r, h):
-        return remote(
-            near.at[r, 0, h], near.at[r, 1, h],
-            sib_sem.at[r, h], near_sem.at[r, 1, h], sibling,
-        )
-
     sends = []
 
-    def start(copy):
+    def pass_on(ry, rz, j, axis, step):
+        place = [ry, rz]
+        place[axis] = (place[axis] - step) % QUAD
+        copy = remote(
+            near.at[ry, rz, j], near.at[place[0], place[1], j],
+            ring_sem.at[len(sends)], near_sem.at[place[0], place[1], j], along(axis, step),
+        )
         copy.start()
         sends.append(copy)
 
-    def prepare(r, k):
+    def handle(far, near_by, j):
+        one, two = (0, 1) if j < 2 else (1, 0)
+        step = 1 - 2 * (j % 2)
+        ry, rz = (far, near_by) if j < 2 else (near_by, far)
+        if far or near_by:
+            arrived(near.at[ry, rz, j], near_sem.at[ry, rz, j])
+        if near_by == 0:
+            if far == 0:
+                pass_on(ry, rz, j, one, 1)
+                pass_on(ry, rz, j, one, -1)
+            elif (far + step) % QUAD == 0:
+                pass_on(ry, rz, j, one, step)
+            pass_on(ry, rz, j, two, 1)
+            pass_on(ry, rz, j, two, -1)
+        elif (near_by + step) % QUAD == 0:
+            pass_on(ry, rz, j, two, step)
+
+    def prepare(ry, rz):
+        r, k = divmod(ry * QUAD + rz, 2)
         for h in range(GRP):
-            block = near[r, k, h]
-            raw = nn(block, wk3[h])
-            scaled = raw * lax.rsqrt(jnp.mean(raw * raw, axis=-1, keepdims=True) + EPS)
+            block = near[ry, rz, :, h].reshape(TOK, HD)
+            flat = nn(block, wk3[h])
+            scaled = flat * lax.rsqrt(jnp.mean(flat * flat, axis=-1, keepdims=True) + EPS)
             keys[h, r * TOK:(r + 1) * TOK, k * HD:(k + 1) * HD] = scaled.astype(BF16)
             vals[h, k * HD:(k + 1) * HD, r * TOK:(r + 1) * TOK] = nt(wvoT[h], block).astype(BF16)
 
-    def sibling_slots(slots):
-        for r in slots:
-            for h in range(GRP):
-                arrived(near.at[r, 1, h], near_sem.at[r, 1, h])
-            prepare(r, 1)
-
-    for d in range(1, QUAD):
-        source = pl.ds(pl.multiple_of(((yh + QUAD - d) % QUAD) * TILE, TILE), TILE)
-        arrived(near.at[0, 0, :, source, :], qr_sem.at[d - 1])
-    for h in range(GRP):
-        if half > 1 or h < 2:
-            start(to_right(0, h))
-        if half > 1 or h == 2:
-            start(to_left(0, h))
-        start(to_sibling(0, h))
+    for d in range(1, QUAD):
+        source = (m + QUAD - d) % QUAD
+        arrived(near.at[0, 0, source], near_sem.at[0, 0, source])
+    for j in (0, 2, 1, 3):
+        handle(0, 0, j)
+
     def sum_to(section, d):
         return remote(
-            sumsq_out, sumsq.at[d], ss_sem.at[d], sr_sem.at[d], at(section, peer(d), z, core)
+            sumsq_out, sumsq.at[d], ss_sem.at[d], sr_sem.at[d], mate(section, d)
         )
 
     def squares(values):
@@ -220,7 +224,7 @@
     def _():
         load_x.wait()
         for d in range(1, QUAD):
-            source = pl.ds(pl.multiple_of(((yh + QUAD - d) % QUAD) * TILE, TILE), TILE)
+            source = pl.ds(pl.multiple_of(((m + QUAD - d) % QUAD) * TILE, TILE), TILE)
             arrived(xin.at[source, :], xr_sem.at[d - 1])
         part = jnp.zeros((8, TOK), F32)
         for h in range(GRP):
@@ -236,33 +240,31 @@
             copy.wait_send()
 
     prepare(0, 0)
-    before = [0]
-    for t in range(1, half + 1):
-        back = nz - t
-        for h in range(GRP):
-            arrived(near.at[back, 0, h], near_sem.at[back, 0, h])
-            if t < half - 1 or (t == half - 1 and h < 2):
-                start(to_right(t, h))
-            start(to_sibling(back, h))
-            if back != t:
-                arrived(near.at[t, 0, h], near_sem.at[t, 0, h])
-                if t < half - 1 or (t == half - 1 and h == 2):
-                    start(to_left(t, h))
-                start(to_sibling(t, h))
-        sibling_slots(before)
-        before = [back] if back == t else [back, t]
-        for r in before:
-            prepare(r, 0)
-    sibling_slots(before)
-
-    for d in range(1, QUAD):
-        source = pl.ds(pl.multiple_of(((yh + QUAD - d) % QUAD) * TILE, TILE), TILE)
+    rounds = (
+        ((1, 0), (3, 0), (0, 1), (0, 3)),
+        ((2, 0), (1, 1), (1, 3), (3, 1), (3, 3), (0, 2)),
+        ((2, 1), (2, 3), (1, 2), (3, 2)),
+        ((2, 2),),
+    )
+    come = {}
+    for steps in rounds:
+        for far, near_by in steps:
+            for j in (0, 2, 1, 3):
+                handle(far, near_by, j)
+                place = (far, near_by) if j < 2 else (near_by, far)
+                come[place] = come.get(place, 0) + 1
+        for place in [p for p in come if come[p] == QUAD]:
+            prepare(*place)
+            del come[place]
+
+    for d in range(1, QUAD):
+        source = pl.ds(pl.multiple_of(((m + QUAD - d) % QUAD) * TILE, TILE), TILE)
         arrived(mask.at[source, :], mr_sem.at[d - 1])
 
     chosen = mask[...].astype(F32)
     keep = jnp.concatenate([1.0 - chosen, jnp.ones_like(chosen)], axis=1)
     zero = jnp.zeros((HD, TOK), BF16)
-    for h in range(GRP):
+    def score(h):
         @pl.when(s > 0)
         def _():
             arrived(ht.at[h], hr_sem.at[h])
@@ -275,6 +277,9 @@
         )
         raw[h] = nn(keys[h], pair)
 
+    for h in range(GRP - 1):
+        score(h)
+
     @pl.when(s > 0)
     def _():
         arrived(sumsq.at[0], sr_sem.at[0])
@@ -288,13 +293,15 @@
     eps = EPS * mean_sq
 
     def hand_on(h):
-        return remote(ot.at[h], ht.at[h], hs_sem.at[h], hr_sem.at[h], at(s + 1, yh, z, core))
+        return remote(ot.at[h], ht.at[h], hs_sem.at[h], hr_sem.at[h], mate(s + 1, 0))
 
     part = jnp.zeros((8, TOK), F32)
     for h in range(GRP):
+        if h == GRP - 1:
+            score(h)
         hidden = ht[h]
         pq, pk, pv = mapped[h, 0:HD], mapped[h, HD:2 * HD], mapped[h, 2 * HD:]
-        scale = scale_ref[0, yh * GRP + h] * (math.log2(math.e) / math.sqrt(HD))
+        scale = scale_ref[0, m * GRP + h] * (math.log2(math.e) / math.sqrt(HD))
         aq = lax.rsqrt(jnp.sum(pq * pq, axis=0, keepdims=True) * (1.0 / HD) + eps) * scale
         bk = lax.rsqrt(jnp.sum(pk * pk, axis=0, keepdims=True) * (1.0 / HD) + eps)
         q = (pq * aq).astype(BF16)
@@ -332,7 +339,7 @@
         theirs = pl.ds(pl.multiple_of(peer(d) * TILE, TILE), TILE)
         outs.append(remote(
             ob.at[theirs, :], out_ref.at[0, :, columns],
-            os_sem.at[d - 1], or_sem.at[d - 1], at(s, peer(d), z, core),
+            os_sem.at[d - 1], or_sem.at[d - 1], mate(s, d),
         ))
         outs[-1].start()
 
@@ -355,7 +362,7 @@
     for d, copy in enumerate(outs, 1):
         copy.wait_send()
         theirs = pl.ds(
-            pl.multiple_of(((yh + QUAD - d) % QUAD) * (GRP * HD), GRP * HD), GRP * HD
+            pl.multiple_of(((m + QUAD - d) % QUAD) * (GRP * HD), GRP * HD), GRP * HD
         )
         arrived(out_ref.at[0, :, theirs], or_sem.at[d - 1])
 
@@ -380,7 +387,7 @@
                 pltpu.VMEM((TILE, FEAT), BF16),
                 pltpu.VMEM((4, GRP, HD, HD), BF16),
                 pltpu.VMEM((QUAD * GRP, TILE, HD), BF16),
-                pltpu.VMEM((nz, 2, GRP, TOK, HD), BF16),
+                pltpu.VMEM((QUAD, QUAD, QUAD, GRP, TILE, HD), BF16),
                 pltpu.VMEM((TOK, TOK), BF16),
                 pltpu.VMEM((TOK, GRP * HD), BF16),
                 pltpu.VMEM((GRP, HD, HD), BF16),
@@ -398,10 +405,9 @@
                 dma((6,)),
                 dma((3,)), dma((3,)),
                 dma((3,)), dma((3,)),
-                dma((3,)), dma((3,)),
-                dma((2, nz // 2, GRP)),
-                dma((nz, GRP)),
-                dma((nz, 2, GRP)),
+                dma((3,)),
+                dma((QUAD * 15,)),
+                dma((QUAD, QUAD, QUAD)),
                 dma((GRP,)), dma((GRP,)),
                 dma((QUAD,)), dma((QUAD,)),
                 dma((3,)), dma((3,)),

time: 92 us -> 84.2 us (0.915)
  Pallas kernels: 90.3 us -> 82.2 us
    pallas_call x1, Pallas kernels: 90.3 us -> 82.2 us  [body(): pl.pallas_call(functools.partial(kernel, sections, nz), out_shape=jax.Sha...]
where the time goes in v3:
time: 84.2 us; the launch traced here: 83.7 us
  Pallas kernels  82.2 us (98%)
  local copies, waits for them, and re-layouts  1.54 us (2%)
    pallas_call x1, Pallas kernels, body(): pl.pallas_call(functools.partial(kernel, sections, nz), out_shape=jax.Sha...  82.2 us

profile of v3, /device:TPU:14, one launch (start us, length us, event | category | flops | bytes accessed | tf_op | source)
XLA Modules:
  0.0 83.7 jit_solution(3090814313461609977)
XLA Ops:
  0.0 82.2 %relay.1 = bf16[1,32,1536]{2,1,0:T(8,128)(2,1)} custom-call(bf16[32,1536]{1,0:T(8,128)(2,1)} %x_ref.1, bf16[1,32,1536]{2,1,0:T(8,128)(2,1)} %stale_ref.1, bf16[1,12,128,128]{3,2,1,0:T(8,128)(2,1)} %wq_ref.1, bf16[1,12,128,128]{3,2,1,0:T(8,128)(2,1)} %wk_ref.1, bf16[1,12,128,128]{3,2,1,0:T(8,128)(2,1)} %wv_ref.1, bf16[1,12,128,128]{3,2,1,0:T(8,128)(2,1)} %wo_ref.1, ...), custom_call_target="tpu_custom_call" | custom-call | tf_op jit(solution)/shard_map/relay/pallas_call | solution.py:378
  82.2 1.5 %copy.10 = bf16[1,32,1536]{2,1,0:T(8,128)(2,1)} copy(bf16[1,32,1536]{2,1,0:T(8,128)(2,1)} %relay.1) | data formatting | bytes 196608

commit v4 on v3

--- a/solution.py
+++ b/solution.py
@@ -41,8 +41,9 @@
     x_ref, stale_ref, wq_ref, wk_ref, wv_ref, wo_ref, scale_ref, assign_ref,
     out_ref,
     stv, wts, normed, near, mask, xin, wk3, wT, wvoT, keys, vals, ht, ot, ob, sumsq, sumsq_out, mapped, raw,
+    tokens, queries, num_sum, den_sum,
     load_sem, xs_sem, xr_sem, ms_sem, mr_sem, qs_sem, ring_sem, near_sem,
-    hs_sem, hr_sem, ss_sem, sr_sem, os_sem, or_sem,
+    hs_sem, hr_sem, ss_sem, sr_sem, os_sem, or_sem, own_sem,
 ):
     s = lax.axis_index("section")
     c = lax.axis_index("ctx")
@@ -61,10 +62,13 @@
     def mate(section, d):
         return at(section, yh, 2 * zh + peer(d) // 2, peer(d) % 2)
 
-    def along(axis, step):
-        if axis == 0:
-            return at(s, (yh + QUAD + step) % QUAD, z, core)
-        return at(s, yh, (z + nz + 2 * step) % nz, core)
+    late = s // (sections // 2)
+
+    def along(axis, step, swap=late):
+        on_y = swap if axis == 0 else 1 - swap
+        return at(
+            s, (yh + QUAD + step * on_y) % QUAD, (z + nz + 2 * step * (1 - on_y)) % nz, core
+        )
 
     first = s == 0
     has_next = s < sections - 1
@@ -170,32 +174,31 @@
 
     sends = []
 
-    def pass_on(ry, rz, j, axis, step):
-        place = [ry, rz]
+    def pass_on(far, near_by, j, axis, step):
+        place = [far, near_by]
         place[axis] = (place[axis] - step) % QUAD
         copy = remote(
-            near.at[ry, rz, j], near.at[place[0], place[1], j],
-            ring_sem.at[len(sends)], near_sem.at[place[0], place[1], j], along(axis, step),
+            near.at[far, near_by, j], near.at[place[0], place[1], j],
+            ring_sem.at[len(sends)], near_sem.at[place[0], place[1], j],
+            along(axis, step, (1 if j == 0 else late)),
         )
         copy.start()
         sends.append(copy)
 
     def handle(far, near_by, j):
-        one, two = (0, 1) if j < 2 else (1, 0)
         step = 1 - 2 * (j % 2)
-        ry, rz = (far, near_by) if j < 2 else (near_by, far)
         if far or near_by:
-            arrived(near.at[ry, rz, j], near_sem.at[ry, rz, j])
+            arrived(near.at[far, near_by, j], near_sem.at[far, near_by, j])
         if near_by == 0:
             if far == 0:
-                pass_on(ry, rz, j, one, 1)
-                pass_on(ry, rz, j, one, -1)
+                pass_on(far, near_by, j, 0, 1)
+                pass_on(far, near_by, j, 0, -1)
             elif (far + step) % QUAD == 0:
-                pass_on(ry, rz, j, one, step)
-            pass_on(ry, rz, j, two, 1)
-            pass_on(ry, rz, j, two, -1)
+                pass_on(far, near_by, j, 0, step)
+            pass_on(far, near_by, j, 1, 1)
+            pass_on(far, near_by, j, 1, -1)
         elif (near_by + step) % QUAD == 0:
-            pass_on(ry, rz, j, two, step)
+            pass_on(far, near_by, j, 1, step)
 
     def prepare(ry, rz):
         r, k = divmod(ry * QUAD + rz, 2)
@@ -206,10 +209,27 @@
             keys[h, r * TOK:(r + 1) * TOK, k * HD:(k + 1) * HD] = scaled.astype(BF16)
             vals[h, k * HD:(k + 1) * HD, r * TOK:(r + 1) * TOK] = nt(wvoT[h], block).astype(BF16)
 
+        @pl.when(first)
+        def _():
+            for h in range(GRP):
+                e = jnp.exp2(nn(keys[h, r * TOK:(r + 1) * TOK, k * HD:(k + 1) * HD], queries[h]))
+                if ry == 0 and rz == 0:
+                    e = e * (1.0 - mask[...].astype(F32))
+                block_den = jnp.sum(e.reshape(TOK // 8, 8, TOK), axis=0)
+                block_num = nn(
+                    vals[h, k * HD:(k + 1) * HD, r * TOK:(r + 1) * TOK], e.astype(BF16)
+                )
+                if ry == 0 and rz == 0:
+                    den_sum[h] = block_den
+                    num_sum[h] = block_num
+                else:
+                    den_sum[h] = den_sum[h] + block_den
+                    num_sum[h] = num_sum[h] + block_num
+
     for d in range(1, QUAD):
         source = (m + QUAD - d) % QUAD
         arrived(near.at[0, 0, source], near_sem.at[0, 0, source])
-    for j in (0, 2, 1, 3):
+    for j in range(QUAD):
         handle(0, 0, j)
 
     def sum_to(section, d):
@@ -233,42 +253,84 @@
             part = part + squares(turned)
         sumsq_out[...] = part
         sumsq[0] = part
-        own = [sum_to(s, d) for d in range(1, QUAD)]
-        for copy in own:
-            copy.start()
-        for copy in own:
-            copy.wait_send()
-
-    prepare(0, 0)
+        for d in range(1, QUAD):
+            sum_to(s, d).start()
+
+    def set_scales():
+        for d in range(1, QUAD):
+            arrived(sumsq.at[d], sr_sem.at[d])
+        total = sumsq[0] + sumsq[1] + sumsq[2] + sumsq[3]
+        mean_sq = jnp.sum(total, axis=0, keepdims=True) * (1.0 / FEAT) + EPS
+        tokens[0:1, :] = lax.rsqrt(mean_sq)
+        tokens[1:2, :] = EPS * mean_sq
+
+    def query_scale(h):
+        pq = mapped[h, 0:HD]
+        scale = scale_ref[0, m * GRP + h] * (math.log2(math.e) / math.sqrt(HD))
+        eps = tokens[1:2, :]
+        return lax.rsqrt(jnp.sum(pq * pq, axis=0, keepdims=True) * (1.0 / HD) + eps) * scale
+
     rounds = (
         ((1, 0), (3, 0), (0, 1), (0, 3)),
         ((2, 0), (1, 1), (1, 3), (3, 1), (3, 3), (0, 2)),
         ((2, 1), (2, 3), (1, 2), (3, 2)),
         ((2, 2),),
     )
-    come = {}
     for steps in rounds:
         for far, near_by in steps:
-            for j in (0, 2, 1, 3):
+            for j in range(QUAD):
                 handle(far, near_by, j)
-                place = (far, near_by) if j < 2 else (near_by, far)
-                come[place] = come.get(place, 0) + 1
-        for place in [p for p in come if come[p] == QUAD]:
-            prepare(*place)
-            del come[place]
-
-    for d in range(1, QUAD):
-        source = pl.ds(pl.multiple_of(((m + QUAD - d) % QUAD) * TILE, TILE), TILE)
-        arrived(mask.at[source, :], mr_sem.at[d - 1])
+        if steps is rounds[0]:
+            for d in range(1, QUAD):
+                source = (m + QUAD - d) % QUAD
+                source = pl.ds(pl.multiple_of(source * TILE, TILE), TILE)
+                arrived(mask.at[source, :], mr_sem.at[d - 1])
+
+            @pl.when(first)
+            def _():
+                set_scales()
+                for d in range(1, QUAD):
+                    sum_to(s, d).wait_send()
+                for h in range(GRP):
+                    mapped[h] = nn(wT[h], ht[h])
+                    queries[h] = (mapped[h, 0:HD] * query_scale(h)).astype(BF16)
+
+            prepare(0, 0)
+        for far, near_by in steps:
+            prepare(far, near_by)
 
     chosen = mask[...].astype(F32)
     keep = jnp.concatenate([1.0 - chosen, jnp.ones_like(chosen)], axis=1)
     zero = jnp.zeros((HD, TOK), BF16)
+
+    def hand_on(h):
+        return remote(ot.at[h], ht.at[h], hs_sem.at[h], hr_sem.at[h], mate(s + 1, 0))
+
+    def out_columns(group, h):
+        return pl.ds(pl.multiple_of(group * (GRP * HD) + h * HD, HD), HD)
+
+    def out_rows(d):
+        return pl.ds(pl.multiple_of(peer(d) * TILE, TILE), TILE)
+
+    def own_out(h):
+        return pltpu.make_async_copy(
+            ob.at[h, mine, :], out_ref.at[0, :, out_columns(m, h)], own_sem.at[h]
+        )
+
+    def out_to(d, h):
+        return remote(
+            ob.at[h, out_rows(d), :], out_ref.at[0, :, out_columns(m, h)],
+            os_sem.at[d - 1, h], or_sem.at[d - 1, h], mate(s, d),
+        )
+
+    def give_out(h):
+        ob[h] = ot[h].astype(F32).T.astype(BF16)
+        for d in (2, 1, 3):
+            out_to(d, h).start()
+        own_out(h).start()
+
     def score(h):
-        @pl.when(s > 0)
-        def _():
-            arrived(ht.at[h], hr_sem.at[h])
-
+        arrived(ht.at[h], hr_sem.at[h])
         both = nn(wT[h], ht[h])
         mapped[h] = both
         p = both[0:HD].astype(BF16)
@@ -277,71 +339,64 @@
         )
         raw[h] = nn(keys[h], pair)
 
-    for h in range(GRP - 1):
-        score(h)
-
-    @pl.when(s > 0)
-    def _():
-        arrived(sumsq.at[0], sr_sem.at[0])
-
-    for d in range(1, QUAD):
-        arrived(sumsq.at[d], sr_sem.at[d])
-
-    total = sumsq[0] + sumsq[1] + sumsq[2] + sumsq[3]
-    mean_sq = jnp.sum(total, axis=0, keepdims=True) * (1.0 / FEAT) + EPS
-    inv = lax.rsqrt(mean_sq)
-    eps = EPS * mean_sq
-
-    def hand_on(h):
-        return remote(ot.at[h], ht.at[h], hs_sem.at[h], hr_sem.at[h], mate(s + 1, 0))
-
-    part = jnp.zeros((8, TOK), F32)
-    for h in range(GRP):
-        if h == GRP - 1:
-            score(h)
-        hidden = ht[h]
-        pq, pk, pv = mapped[h, 0:HD], mapped[h, HD:2 * HD], mapped[h, 2 * HD:]
-        scale = scale_ref[0, m * GRP + h] * (math.log2(math.e) / math.sqrt(HD))
-        aq = lax.rsqrt(jnp.sum(pq * pq, axis=0, keepdims=True) * (1.0 / HD) + eps) * scale
-        bk = lax.rsqrt(jnp.sum(pk * pk, axis=0, keepdims=True) * (1.0 / HD) + eps)
-        q = (pq * aq).astype(BF16)
-        kf = (pk * bk).astype(BF16)
-        vf = (pv * inv).astype(BF16)
+    def stale_part(h):
+        aq = query_scale(h)
         e = jnp.exp2(raw[h] * jnp.concatenate([aq, aq], axis=1))
         e = jnp.concatenate([e[0:TOK] * keep, e[TOK:]], axis=0)
+        den = jnp.sum(e.reshape(nz * TOK // 8, 8, 2 * TOK), axis=0)
+        both = nn(vals[h], e.astype(BF16))
+        return both[0:HD, 0:TOK] + both[HD:, TOK:], den[:, :TOK] + den[:, TOK:]
+
+    def finish(h, numer, den):
+        pq, pk, pv = mapped[h, 0:HD], mapped[h, HD:2 * HD], mapped[h, 2 * HD:]
+        eps = tokens[1:2, :]
+        bk = lax.rsqrt(jnp.sum(pk * pk, axis=0, keepdims=True) * (1.0 / HD) + eps)
+        q = (pq * query_scale(h)).astype(BF16)
+        kf = (pk * bk).astype(BF16)
+        vf = (pv * tokens[0:1, :]).astype(BF16)
         e_new = jnp.exp2(tn(kf, q)) * chosen
-        den = jnp.sum(e.reshape(nz * TOK // 8, 8, 2 * TOK), axis=0)
-        den = den[:, :TOK] + den[:, TOK:] + jnp.sum(e_new.reshape(TOK // 8, 8, TOK), axis=0)
+        den = den + jnp.sum(e_new.reshape(TOK // 8, 8, TOK), axis=0)
         den = jnp.sum(den, axis=0, keepdims=True)
-        both = nn(vals[h], e.astype(BF16))
-        numer = both[0:HD, 0:TOK] + both[HD:, TOK:] + nn(vf, e_new.astype(BF16))
-        result = (hidden.astype(F32) + numer * (1.0 / den)).astype(BF16)
+        numer = numer + nn(vf, e_new.astype(BF16))
+        result = (ht[h].astype(F32) + numer * (1.0 / den)).astype(BF16)
         ot[h] = result
+        part = squares(result.astype(F32))
+        if h == 0:
+            sumsq_out[...] = part
+        else:
+            sumsq_out[...] = sumsq_out[...] + part
 
         @pl.when(has_next)
         def _():
             hand_on(h).start()
-
-        part = part + squares(result.astype(F32))
+            if h == GRP - 1:
+                for d in (2, 1, 3, 0):
+                    sum_to(s + 1, d).start()
+
+    @pl.when(first)
+    def _():
+        for h in range(GRP):
+            finish(h, num_sum[h], den_sum[h])
+
+    @pl.when(s > 0)
+    def _():
+        for h in range(GRP - 1):
+            score(h)
+        arrived(sumsq.at[0], sr_sem.at[0])
+        set_scales()
+        for h in range(GRP):
+            if h == GRP - 1:
+                score(h)
+            finish(h, *stale_part(h))
+
+            @pl.when(jnp.logical_not(has_next))
+            def _():
+                give_out(h)
 
     @pl.when(has_next)
     def _():
-        sumsq_out[...] = part
-        for d in (2, 1, 3, 0):
-            sum_to(s + 1, d).start()
-
-    for h in range(GRP):
-        ob[:, h * HD:(h + 1) * HD] = ot[h].astype(F32).T.astype(BF16)
-    own_out = pltpu.make_async_copy(ob.at[mine, :], out_ref.at[0, :, columns], load_sem.at[0])
-    own_out.start()
-    outs = []
-    for d in range(1, QUAD):
-        theirs = pl.ds(pl.multiple_of(peer(d) * TILE, TILE), TILE)
-        outs.append(remote(
-            ob.at[theirs, :], out_ref.at[0, :, columns],
-            os_sem.at[d - 1], or_sem.at[d - 1], mate(s, d),
-        ))
-        outs[-1].start()
+        for h in range(GRP):
+            give_out(h)
 
     for copy in sends + quad_sends + mask_sends:
         copy.wait_send()
@@ -358,13 +413,12 @@
         for d in range(QUAD):
             sum_to(s + 1, d).wait_send()
 
-    own_out.wait()
-    for d, copy in enumerate(outs, 1):
-        copy.wait_send()
-        theirs = pl.ds(
-            pl.multiple_of(((m + QUAD - d) % QUAD) * (GRP * HD), GRP * HD), GRP * HD
-        )
-        arrived(out_ref.at[0, :, theirs], or_sem.at[d - 1])
+    for h in range(GRP):
+        own_out(h).wait()
+        for d in range(1, QUAD):
+            out_to(d, h).wait_send()
+            theirs = out_columns((m + QUAD - d) % QUAD, h)
+            arrived(out_ref.at[0, :, theirs], or_sem.at[d - 1, h])
 
 
 def solution(mesh):
@@ -397,11 +451,15 @@
                 pltpu.VMEM((GRP, 2 * HD, keys), BF16),
                 pltpu.VMEM((GRP, HD, TOK), BF16),
                 pltpu.VMEM((GRP, HD, TOK), BF16),
-                pltpu.VMEM((TOK, GRP * HD), BF16),
+                pltpu.VMEM((GRP, TOK, HD), BF16),
                 pltpu.VMEM((QUAD, 8, TOK), F32),
                 pltpu.VMEM((8, TOK), F32),
                 pltpu.VMEM((GRP, 3 * HD, TOK), F32),
                 pltpu.VMEM((GRP, keys, 2 * TOK), F32),
+                pltpu.VMEM((8, TOK), F32),
+                pltpu.VMEM((GRP, HD, TOK), BF16),
+                pltpu.VMEM((GRP, HD, TOK), F32),
+                pltpu.VMEM((GRP, 8, TOK), F32),
                 dma((6,)),
                 dma((3,)), dma((3,)),
                 dma((3,)), dma((3,)),
@@ -410,7 +468,7 @@
                 dma((QUAD, QUAD, QUAD)),
                 dma((GRP,)), dma((GRP,)),
                 dma((QUAD,)), dma((QUAD,)),
-                dma((3,)), dma((3,)),
+                dma((3, GRP)), dma((3, GRP)), dma((GRP,)),
             ],
             compiler_params=pltpu.CompilerParams(
                 collective_id=0, has_side_effects=True, vmem_limit_bytes=60 * 2**20

time: 84.2 us -> 80.8 us (0.960)
  Pallas kernels: 82.2 us -> 78.8 us
    pallas_call x1, Pallas kernels: 82.2 us -> 78.8 us  [body(): pl.pallas_call(functools.partial(kernel, sections, nz), out_shape=jax.Sha...]
where the time goes in v4:
time: 80.8 us; the launch traced here: 80.3 us
  Pallas kernels  78.8 us (98%)
  local copies, waits for them, and re-layouts  1.54 us (2%)
    pallas_call x1, Pallas kernels, body(): pl.pallas_call(functools.partial(kernel, sections, nz), out_shape=jax.Sha...  78.8 us

profile of v4, /device:TPU:14, one launch (start us, length us, event | category | flops | bytes accessed | tf_op | source)
XLA Modules:
  0.0 80.3 jit_solution(1736855942009602723)
XLA Ops:
  0.0 78.8 %relay.1 = bf16[1,32,1536]{2,1,0:T(8,128)(2,1)} custom-call(bf16[32,1536]{1,0:T(8,128)(2,1)} %x_ref.1, bf16[1,32,1536]{2,1,0:T(8,128)(2,1)} %stale_ref.1, bf16[1,12,128,128]{3,2,1,0:T(8,128)(2,1)} %wq_ref.1, bf16[1,12,128,128]{3,2,1,0:T(8,128)(2,1)} %wk_ref.1, bf16[1,12,128,128]{3,2,1,0:T(8,128)(2,1)} %wv_ref.1, bf16[1,12,128,128]{3,2,1,0:T(8,128)(2,1)} %wo_ref.1, ...), custom_call_target="tpu_custom_call" | custom-call | tf_op jit(solution)/shard_map/relay/pallas_call | solution.py:432
  78.8 1.5 %copy.10 = bf16[1,32,1536]{2,1,0:T(8,128)(2,1)} copy(bf16[1,32,1536]{2,1,0:T(8,128)(2,1)} %relay.1) | data formatting | bytes 196608

commit v5 on v4

--- a/solution.py
+++ b/solution.py
@@ -174,31 +174,33 @@
 
     sends = []
 
-    def pass_on(far, near_by, j, axis, step):
+    def pass_on(far, near_by, d, axis, step):
+        j = (m + QUAD - d) % QUAD
         place = [far, near_by]
         place[axis] = (place[axis] - step) % QUAD
         copy = remote(
             near.at[far, near_by, j], near.at[place[0], place[1], j],
             ring_sem.at[len(sends)], near_sem.at[place[0], place[1], j],
-            along(axis, step, (1 if j == 0 else late)),
+            along(axis, step, (1 if d == 0 else late)),
         )
         copy.start()
         sends.append(copy)
 
-    def handle(far, near_by, j):
-        step = 1 - 2 * (j % 2)
-        if far or near_by:
+    def handle(far, near_by, d):
+        j = (m + QUAD - d) % QUAD
+        step = 1 - 2 * (d % 2)
+        if far or near_by or d:
             arrived(near.at[far, near_by, j], near_sem.at[far, near_by, j])
         if near_by == 0:
             if far == 0:
-                pass_on(far, near_by, j, 0, 1)
-                pass_on(far, near_by, j, 0, -1)
+                pass_on(far, near_by, d, 0, 1)
+                pass_on(far, near_by, d, 0, -1)
             elif (far + step) % QUAD == 0:
-                pass_on(far, near_by, j, 0, step)
-            pass_on(far, near_by, j, 1, 1)
-            pass_on(far, near_by, j, 1, -1)
+                pass_on(far, near_by, d, 0, step)
+            pass_on(far, near_by, d, 1, 1)
+            pass_on(far, near_by, d, 1, -1)
         elif (near_by + step) % QUAD == 0:
-            pass_on(far, near_by, j, 1, step)
+            pass_on(far, near_by, d, 1, step)
 
     def prepare(ry, rz):
         r, k = divmod(ry * QUAD + rz, 2)
@@ -226,11 +228,8 @@
                     den_sum[h] = den_sum[h] + block_den
                     num_sum[h] = num_sum[h] + block_num
 
-    for d in range(1, QUAD):
-        source = (m + QUAD - d) % QUAD
-        arrived(near.at[0, 0, source], near_sem.at[0, 0, source])
-    for j in range(QUAD):
-        handle(0, 0, j)
+    for d in (0, 1, 3, 2):
+        handle(0, 0, d)
 
     def sum_to(section, d):
         return remote(
@@ -238,7 +237,7 @@
         )
 
     def squares(values):
-        return jnp.sum((values * values).reshape(HD // 8, 8, TOK), axis=0)
+        return jnp.sum(values * values, axis=0, keepdims=True)
 
     @pl.when(first)
     def _():
@@ -246,7 +245,7 @@
         for d in range(1, QUAD):
             source = pl.ds(pl.multiple_of(((m + QUAD - d) % QUAD) * TILE, TILE), TILE)
             arrived(xin.at[source, :], xr_sem.at[d - 1])
-        part = jnp.zeros((8, TOK), F32)
+        part = jnp.zeros((1, TOK), F32)
         for h in range(GRP):
             turned = xin[:, h * HD:(h + 1) * HD].astype(F32).T
             ht[h] = turned.astype(BF16)
@@ -260,7 +259,7 @@
         for d in range(1, QUAD):
             arrived(sumsq.at[d], sr_sem.at[d])
         total = sumsq[0] + sumsq[1] + sumsq[2] + sumsq[3]
-        mean_sq = jnp.sum(total, axis=0, keepdims=True) * (1.0 / FEAT) + EPS
+        mean_sq = total * (1.0 / FEAT) + EPS
         tokens[0:1, :] = lax.rsqrt(mean_sq)
         tokens[1:2, :] = EPS * mean_sq
 
@@ -278,8 +277,8 @@
     )
     for steps in rounds:
         for far, near_by in steps:
-            for j in range(QUAD):
-                handle(far, near_by, j)
+            for d in (0, 1, 3, 2):
+                handle(far, near_by, d)
         if steps is rounds[0]:
             for d in range(1, QUAD):
                 source = (m + QUAD - d) % QUAD
@@ -368,10 +367,10 @@
 
         @pl.when(has_next)
         def _():
-            hand_on(h).start()
             if h == GRP - 1:
                 for d in (2, 1, 3, 0):
                     sum_to(s + 1, d).start()
+            hand_on(h).start()
 
     @pl.when(first)
     def _():
@@ -452,8 +451,8 @@
                 pltpu.VMEM((GRP, HD, TOK), BF16),
                 pltpu.VMEM((GRP, HD, TOK), BF16),
                 pltpu.VMEM((GRP, TOK, HD), BF16),
-                pltpu.VMEM((QUAD, 8, TOK), F32),
-                pltpu.VMEM((8, TOK), F32),
+                pltpu.VMEM((QUAD, 1, TOK), F32),
+                pltpu.VMEM((1, TOK), F32),
                 pltpu.VMEM((GRP, 3 * HD, TOK), F32),
                 pltpu.VMEM((GRP, keys, 2 * TOK), F32),
                 pltpu.VMEM((8, TOK), F32),

time: 80.8 us -> 78.1 us (0.967)
  Pallas kernels: 78.8 us -> 76.1 us
    pallas_call x1, Pallas kernels: 78.8 us -> 76.1 us  [body(): pl.pallas_call(functools.partial(kernel, sections, nz), out_shape=jax.Sha...]
where the time goes in v5:
time: 78.1 us; the launch traced here: 77.7 us
  Pallas kernels  76.1 us (97%)
  local copies, waits for them, and re-layouts  1.54 us (2%)
    pallas_call x1, Pallas kernels, body(): pl.pallas_call(functools.partial(kernel, sections, nz), out_shape=jax.Sha...  76.1 us

profile of v5, /device:TPU:14, one launch (start us, length us, event | category | flops | bytes accessed | tf_op | source)
XLA Modules:
  0.0 77.7 jit_solution(5203243151066124187)
XLA Ops:
  0.0 76.1 %relay.1 = bf16[1,32,1536]{2,1,0:T(8,128)(2,1)} custom-call(bf16[32,1536]{1,0:T(8,128)(2,1)} %x_ref.1, bf16[1,32,1536]{2,1,0:T(8,128)(2,1)} %stale_ref.1, bf16[1,12,128,128]{3,2,1,0:T(8,128)(2,1)} %wq_ref.1, bf16[1,12,128,128]{3,2,1,0:T(8,128)(2,1)} %wk_ref.1, bf16[1,12,128,128]{3,2,1,0:T(8,128)(2,1)} %wv_ref.1, bf16[1,12,128,128]{3,2,1,0:T(8,128)(2,1)} %wo_ref.1, ...), custom_call_target="tpu_custom_call" | custom-call | tf_op jit(solution)/shard_map/relay/pallas_call | solution.py:431
  76.1 1.5 %copy.10 = bf16[1,32,1536]{2,1,0:T(8,128)(2,1)} copy(bf16[1,32,1536]{2,1,0:T(8,128)(2,1)} %relay.1) | data formatting | bytes 196608

commit v6 on v5

--- a/solution.py
+++ b/solution.py
@@ -161,17 +161,6 @@
     for copy in mask_sends:
         copy.start()
 
-    for copy in loads:
-        copy.wait()
-    for h in range(GRP):
-        wk = wts[0, h]
-        wk3[h] = wk
-        wvo = nn(wts[2, h], wts[3, h]).T.astype(BF16)
-        wvoT[h] = wvo
-        wT[h, 0:HD, :] = wts[1, h].astype(F32).T.astype(BF16)
-        wT[h, HD:2 * HD, :] = wk.astype(F32).T.astype(BF16)
-        wT[h, 2 * HD:, :] = wvo
-
     sends = []
 
     def pass_on(far, near_by, d, axis, step):
@@ -230,6 +219,17 @@
 
     for d in (0, 1, 3, 2):
         handle(0, 0, d)
+
+    for copy in loads:
+        copy.wait()
+    for h in range(GRP):
+        wk = wts[0, h]
+        wk3[h] = wk
+        wvo = nn(wts[2, h], wts[3, h]).T.astype(BF16)
+        wvoT[h] = wvo
+        wT[h, 0:HD, :] = wts[1, h].astype(F32).T.astype(BF16)
+        wT[h, HD:2 * HD, :] = wk.astype(F32).T.astype(BF16)
+        wT[h, 2 * HD:, :] = wvo
 
     def sum_to(section, d):
         return remote(

time: 78.1 us -> 77.4 us (level)
  the two profiles are of different devices: /device:TPU:14 before, /device:TPU:31 now
where the time goes in v6:
time: 77.4 us; the launch traced here: 77.2 us
  Pallas kernels  75.7 us (98%)
  local copies, waits for them, and re-layouts  1.54 us (2%)
    pallas_call x1, Pallas kernels, body(): pl.pallas_call(functools.partial(kernel, sections, nz), out_shape=jax.Sha...  75.7 us

profile of v6, /device:TPU:31, one launch (start us, length us, event | category | flops | bytes accessed | tf_op | source)
XLA Modules:
  0.0 77.2 jit_solution(8001510079785889670)
XLA Ops:
  0.0 75.7 %relay.1 = bf16[1,32,1536]{2,1,0:T(8,128)(2,1)} custom-call(bf16[32,1536]{1,0:T(8,128)(2,1)} %x_ref.1, bf16[1,32,1536]{2,1,0:T(8,128)(2,1)} %stale_ref.1, bf16[1,12,128,128]{3,2,1,0:T(8,128)(2,1)} %wq_ref.1, bf16[1,12,128,128]{3,2,1,0:T(8,128)(2,1)} %wk_ref.1, bf16[1,12,128,128]{3,2,1,0:T(8,128)(2,1)} %wv_ref.1, bf16[1,12,128,128]{3,2,1,0:T(8,128)(2,1)} %wo_ref.1, ...), custom_call_target="tpu_custom_call" | custom-call | tf_op jit(solution)/shard_map/relay/pallas_call | solution.py:431
  75.7 1.5 %copy.10 = bf16[1,32,1536]{2,1,0:T(8,128)(2,1)} copy(bf16[1,32,1536]{2,1,0:T(8,128)(2,1)} %relay.1) | data formatting | bytes 196608

commit v7 on v6

--- a/solution.py
+++ b/solution.py
@@ -181,13 +181,13 @@
         if far or near_by or d:
             arrived(near.at[far, near_by, j], near_sem.at[far, near_by, j])
         if near_by == 0:
+            pass_on(far, near_by, d, 1, 1)
+            pass_on(far, near_by, d, 1, -1)
             if far == 0:
                 pass_on(far, near_by, d, 0, 1)
                 pass_on(far, near_by, d, 0, -1)
             elif (far + step) % QUAD == 0:
                 pass_on(far, near_by, d, 0, step)
-            pass_on(far, near_by, d, 1, 1)
-            pass_on(far, near_by, d, 1, -1)
         elif (near_by + step) % QUAD == 0:
             pass_on(far, near_by, d, 1, step)
 

time: 77.4 us -> 77.4 us (level)
  no operation moved by 1% of the time
where the time goes in v7:
time: 77.4 us; the launch traced here: 77.2 us
  Pallas kernels  75.7 us (98%)
  local copies, waits for them, and re-layouts  1.54 us (2%)
    pallas_call x1, Pallas kernels, body(): pl.pallas_call(functools.partial(kernel, sections, nz), out_shape=jax.Sha...  75.7 us

profile of v7, /device:TPU:31, one launch (start us, length us, event | category | flops | bytes accessed | tf_op | source)
XLA Modules:
  0.0 77.2 jit_solution(17255930910979537808)
XLA Ops:
  0.0 75.7 %relay.1 = bf16[1,32,1536]{2,1,0:T(8,128)(2,1)} custom-call(bf16[32,1536]{1,0:T(8,128)(2,1)} %x_ref.1, bf16[1,32,1536]{2,1,0:T(8,128)(2,1)} %stale_ref.1, bf16[1,12,128,128]{3,2,1,0:T(8,128)(2,1)} %wq_ref.1, bf16[1,12,128,128]{3,2,1,0:T(8,128)(2,1)} %wk_ref.1, bf16[1,12,128,128]{3,2,1,0:T(8,128)(2,1)} %wv_ref.1, bf16[1,12,128,128]{3,2,1,0:T(8,128)(2,1)} %wo_ref.1, ...), custom_call_target="tpu_custom_call" | custom-call | tf_op jit(solution)/shard_map/relay/pallas_call | solution.py:431
  75.7 1.5 %copy.10 = bf16[1,32,1536]{2,1,0:T(8,128)(2,1)} copy(bf16[1,32,1536]{2,1,0:T(8,128)(2,1)} %relay.1) | data formatting | bytes 196608
